TPU v7x, 32 devices: a whole 2x2x4 slice. The times are simulated.
32 devices in a mesh: seq: 8 (over z, y), grp: 4 (over x, core).
Axes of the slice: x: 2, y: 2, z: 4, core: 2. Of those that a mesh axis runs over, the one named last changes fastest.
Arguments:
- q_nope: bfloat16 [128, 128, 128], P('seq', 'grp'), may hold values from -6 to 6
- q_rope: bfloat16 [128, 128, 64], P('seq', 'grp'), may hold values from -256 to 256
- cache: bfloat16 [8192, 576], P('seq'), may hold values from -6 to 6
- w_uk: bfloat16 [128, 65536], P('grp', 'seq'), may hold values from -0.5 to 0.5
- w_uv: bfloat16 [128, 65536], P('grp', 'seq'), may hold values from -0.25 to 0.25
- d_out: bfloat16 [128, 128, 128], P('seq', 'grp'), may hold values from -6 to 6
- sel: int32 [128, 32], P('seq'), may hold values from 0 to 63, as said below
- slot_blocks: int32 [8, 64], P('seq'), may hold values from 0 to 15, as said below
Outputs:
- attn_out: bfloat16 [128, 128, 128], P('seq', 'grp')
- d_q_nope: bfloat16 [128, 128, 128], P('seq', 'grp')
- d_q_rope: bfloat16 [128, 128, 64], P('seq', 'grp')
- d_cache: float32 [8192, 576], P('seq')
Inputs may be any that keep to these rules, and one draw needn't show every extreme that they name: `sel`: each row names 32 different places; place s stands for the block that the row's device asks of device s // 8. `slot_blocks`: entry [r, s] is the index among device s // 8's own blocks of the block that device r asks for in place s; the 8 entries of a row toward one device differ.
All inputs are finite; a program needn't handle non-finite values.
Results may differ from a plain program's by a relative error of at most 0.015.
Values may be sent and summed in bfloat16 or wider, within the bound.
No kernel may reach another device: no remote copies, remote signals or barrier semaphores. Data moves between devices by JAX's collectives and lax.ppermute only.
A program may use at most 128 MiB of HBM per device.

v0:
```python
import functools
import math

import jax
import jax.numpy as jnp
from jax import lax
from jax.experimental import pallas as pl
from jax.experimental.pallas import tpu as pltpu
from jax.sharding import PartitionSpec as P

BLOCK_LEN = 64
LANES = 128
HIDDEN = -1e30
VMEM = pl.BlockSpec(memory_space=pltpu.VMEM)
SMEM = pl.BlockSpec(memory_space=pltpu.SMEM)
ANY = pl.BlockSpec(memory_space=pl.ANY)
F32 = jnp.float32
BF16 = jnp.bfloat16


def call(kernel, name, args, specs, outs, scratch=(), mib=32, tied=None):
    out_shape = [jax.ShapeDtypeStruct(s, d) for s, d in outs]
    out_specs = [VMEM] * len(outs)
    aliases = {}
    body = kernel
    if tied is not None:
        args, specs = (tied, *args), [ANY] + specs
        out_shape, out_specs = [jax.ShapeDtypeStruct(tied.shape, tied.dtype)] + out_shape, [ANY] + out_specs
        aliases = {0: 0}
        n_in = len(args)

        def body(*refs):
            kernel(*refs[1:n_in], *refs[n_in + 1 :])

    return pl.pallas_call(
        body,
        out_shape=out_shape,
        in_specs=specs,
        out_specs=out_specs,
        scratch_shapes=list(scratch),
        input_output_aliases=aliases,
        compiler_params=pltpu.CompilerParams(vmem_limit_bytes=mib * 2**20),
        name=name,
    )(*args)


def nt(a, b):
    return lax.dot_general(a, b, (((1,), (1,)), ((), ())), preferred_element_type=F32)


def nn(a, b):
    return lax.dot_general(a, b, (((1,), (0,)), ((), ())), preferred_element_type=F32)


def swap(x, axis, bit):
    n = lax.axis_size(axis)
    return lax.ppermute(x, axis, [(i, i ^ bit) for i in range(n)])


def seq_swap(x):
    return lax.all_to_all(x, "seq", split_axis=0, concat_axis=0, tiled=True)


def exchange(pieces):
    return [pieces[0]] + [swap(p, "seq", k) for k, p in enumerate(pieces) if k > 0]


def cut_kernel(ids, cache, out):
    depth = out.shape[0]
    out[...] = cache[pl.ds(pl.multiple_of(ids[1] * depth, 16), depth), :]


def gather_kernel(per_peer, ids, own, other, *refs):
    owners = len(refs) - 2
    caches, outs = refs[:owners], refs[owners:]
    lanes = per_peer * BLOCK_LEN

    def block(row, i, j):
        b = row[0, (ids[0] ^ (2 * i)) * per_peer + j]
        tile = caches[i][:, pl.ds(pl.multiple_of((b >> 1) * LANES, LANES), LANES)]
        return jnp.where((b & 1) == 1, tile[:, BLOCK_LEN:], tile[:, :BLOCK_LEN])

    for row, out in zip((other, own), outs):
        for i in range(owners):
            for j in range(0, per_peer, 2):
                both = jnp.concatenate([block(row, i, j), block(row, i, j + 1)], axis=1)
                at = i * lanes + j * BLOCK_LEN
                out[:, at : at + 2 * BLOCK_LEN] = both


def scatter_kernel(count, ids, rows, *refs):
    got, out, acc = refs[:count], refs[count], refs[count + 1]
    me = ids[0]
    depth, lanes = got[0].shape
    per_peer = lanes // BLOCK_LEN
    acc[...] = jnp.zeros_like(acc)
    blank = jnp.zeros((depth, BLOCK_LEN), F32)
    for k in range(count):
        for j in range(per_peer):
            b = rows[k, me * per_peer + j]
            at = pl.ds(pl.multiple_of((b >> 1) * LANES, LANES), LANES)
            g = got[k][:, j * BLOCK_LEN : (j + 1) * BLOCK_LEN].astype(F32)
            low = jnp.concatenate([g, blank], axis=1)
            high = jnp.concatenate([blank, g], axis=1)
            acc[:, at] = acc[:, at] + jnp.where((b & 1) == 1, high, low)
    out[...] = acc[...].astype(BF16)


def assemble_kernel(ids, *refs):
    parts, out = refs[:-1], refs[-1]
    depth = parts[0].shape[0]
    for k, y in enumerate(parts):
        out[pl.ds(pl.multiple_of((ids[1] ^ k) * depth, 16), depth), :] = y[...].astype(F32)


def weight_k_of(pack, head, uk_rows, tiles):
    rows = uk_rows // tiles
    peers = pack.shape[0]
    cols = []
    for t in range(tiles):
        cols.append(
            jnp.concatenate(
                [pack[r, head, t * rows : (t + 1) * rows, :] for r in range(peers)], axis=0
            )
        )
    return jnp.concatenate(cols, axis=1)


def stacked(pack, head, start, rows):
    peers = pack.shape[0]
    return jnp.concatenate([pack[r, head, start : start + rows, :] for r in range(peers)], axis=0)


def expand_kernel(sizes, pack, out):
    uk_rows, uv_rows, queries, tiles, latent = sizes
    peers, heads = pack.shape[0], pack.shape[1]
    for h in range(heads):
        wk = weight_k_of(pack, h, uk_rows, tiles)
        wv = stacked(pack, h, uk_rows, uv_rows)
        qn = stacked(pack, h, uk_rows + uv_rows, queries)
        do = stacked(pack, h, uk_rows + uv_rows + queries, queries)
        q_lat = nn(qn, wk).astype(BF16)
        d_olat = nt(do, wv).astype(BF16)
        for r in range(peers):
            out[r, h, :, :latent] = q_lat[r * queries : (r + 1) * queries]
            out[r, h, :, latent:] = d_olat[r * queries : (r + 1) * queries]


def reduce_kernel(sizes, pack, lat, out):
    uk_rows, uv_rows, queries, tiles, latent = sizes
    peers, heads = pack.shape[0], pack.shape[1]
    for h in range(heads):
        wk = weight_k_of(pack, h, uk_rows, tiles)
        wv = stacked(pack, h, uk_rows, uv_rows)
        both = jnp.concatenate([lat[r, h] for r in range(peers)], axis=0)
        attn = nn(both[:, :latent], wv).astype(BF16)
        dqn = nt(both[:, latent:], wk).astype(BF16)
        for r in range(peers):
            out[r, h, :, : attn.shape[1]] = attn[r * queries : (r + 1) * queries]
            out[r, h, :, attn.shape[1] :] = dqn[r * queries : (r + 1) * queries]


def far_or_near(grads, scale, do, cat, delta, kt, p, width):
    keep, send, at, depth = grads
    latent = do.shape[1]
    dp = nn(do[...], kt[:latent])
    ds = (p.astype(F32) * (dp - delta) * scale).astype(BF16)
    part = nt(ds, kt[:width])
    dk = nn(cat[...], jnp.concatenate([ds, p], axis=0)).astype(BF16)
    for k, ref in enumerate((keep, send, keep, send)):
        ref[k // 2, :, at] = dk[k * depth : (k + 1) * depth]
    return part


def first_kernel(scale, per_peer, ids, sel, rope, qd, *refs):
    keys, refs = (refs[:4], refs[4:8]), refs[8:]
    kt_near, pb_near, cat, o_lat, delta_out, keep, send, dq, refs = (*refs[:8], refs[8:])
    kt_far, pb_far, qx, do, sc, flip, o_full = refs
    rows, latent = do.shape
    heads, queries, rope_dim = rope.shape
    width = latent + rope_dim
    slots = qx.shape[1] - width
    depth, half = keys[0][0].shape
    held = 4
    lanes = half // held
    kts, pbs = (kt_near, kt_far), (pb_near, pb_far)

    picks = sel[...] ^ (ids[0] * per_peer)
    slot = lax.broadcasted_iota(jnp.int32, (queries, slots), 1)
    chosen = picks[:, 0:1] == slot
    for j in range(1, picks.shape[1]):
        chosen = chosen | (picks[:, j : j + 1] == slot)
    bias = jnp.where(chosen, 0.0, HIDDEN).astype(BF16)
    bias = jnp.broadcast_to(bias[None], (heads, queries, slots)).reshape(rows, slots)
    qx[:, :latent] = qd[:, :latent]
    qx[:, latent:] = jnp.concatenate([rope[...].reshape(rows, rope_dim), bias], axis=1)
    do[...] = qd[:, latent:]
    for c in range(2):
        for k in range(4):
            at = pl.ds(pl.multiple_of((ids[1] ^ k) * depth, 16), depth)
            for i in range(held):
                peer = c * held + i
                src = keys[peer % 2][k][:, (peer // 2) * lanes : (peer // 2 + 1) * lanes]
                kts[c][at, i * lanes : (i + 1) * lanes] = src
        place = lax.broadcasted_iota(jnp.int32, (slots, half), 0)
        token = lax.broadcasted_iota(jnp.int32, (slots, half), 1) + c * half
        kts[c][width:, :] = jnp.where(token // BLOCK_LEN == place, 1.0, 0.0).astype(BF16)

    scale2 = scale * math.log2(math.e)
    step = 512
    chunks = [(c, i) for c in range(2) for i in range(0, half, step)]
    top = jnp.full((rows, 1), -jnp.inf, F32)
    for n, (c, i) in enumerate(chunks):
        s = nn(qx[...], kts[c][:, i : i + step]) * scale2
        sc[:, n * step : (n + 1) * step] = s
        top = jnp.maximum(top, jnp.max(s, axis=1, keepdims=True))
    total = jnp.zeros((rows, 1), F32)
    for n in range(len(chunks)):
        e = jnp.exp2(sc[:, n * step : (n + 1) * step] - top)
        sc[:, n * step : (n + 1) * step] = e
        total = total + jnp.sum(e, axis=1, keepdims=True)
    inv = 1.0 / total
    for n, (c, i) in enumerate(chunks):
        pb = (sc[:, n * step : (n + 1) * step] * inv).astype(BF16)
        pbs[c][:, i : i + step] = pb
        part = nt(pb, kts[c][:latent, i : i + step])
        if n == 0:
            o_full[...] = part
        else:
            o_full[...] += part
    o_lat[...] = o_full[...].astype(BF16)
    delta = jnp.sum(o_full[...] * do[...].astype(F32), axis=1, keepdims=True)
    delta_out[...] = delta

    flip[:, :rows] = qx[:, :width].T
    flip[:latent, rows:] = do[...].T
    flip[latent:, rows:] = jnp.zeros((rope_dim, rows), BF16)
    for k in range(4):
        at = pl.ds(pl.multiple_of((ids[1] ^ k) * depth, 16), depth)
        cat[k * depth : (k + 1) * depth] = flip[at, :]
    for i in range(0, half, step):
        at = slice(i, i + step)
        grads = (keep, send, at, depth)
        part = far_or_near(grads, scale, do, cat, delta, kt_far.at[:, at], pb_far[:, at], width)
        if i == 0:
            dq[...] = part
        else:
            dq[...] += part


def second_kernel(scale, qd, cat, delta, kt, pb, o_lat, before, keep, send, lat, d_rope, do, dq):
    rows, latent = do.shape
    width = cat.shape[0]
    depth = width // 4
    do[...] = qd[:, latent:]
    step = 512
    dq[...] = before[...]
    for i in range(0, pb.shape[1], step):
        at = slice(i, i + step)
        grads = (keep, send, at, depth)
        dq[...] += far_or_near(
            grads, scale, do, cat, delta[...], kt.at[:, at], pb[:, at], width
        )
    lat[:, :latent] = o_lat[...]
    lat[:, latent:] = dq[:, :latent].astype(BF16)
    d_rope[...] = dq[:, latent:].astype(BF16)


def pair_kernel(keep, got, a0, *a2):
    total = keep[...].astype(F32) + got[...].astype(F32)
    a0[...] = total[0].astype(BF16)
    lanes = a2[0].shape[1]
    for i, a in enumerate(a2):
        a[...] = total[1, :, i * lanes : (i + 1) * lanes].astype(BF16)


def owner_kernel(a0, got, *outs):
    total = (a0[...].astype(F32) + got[...].astype(F32)).astype(BF16)
    lanes = outs[0].shape[1]
    for i, out in enumerate(outs):
        out[...] = total[:, i * lanes : (i + 1) * lanes]


def local(q_nope, q_rope, cache, w_uk, w_uv, d_out, sel, slot_blocks):
    peers = lax.axis_size("seq")
    groups = lax.axis_size("grp")
    queries, heads, nope = q_nope.shape
    rope = q_rope.shape[2]
    width = cache.shape[1]
    latent = width - rope
    value = d_out.shape[2]
    slots = slot_blocks.shape[1]
    per_peer = slots // peers
    if not (peers == 8 and groups == 4 and heads % peers == 0 and per_peer % 2 == 0):
        return local_general(q_nope, q_rope, cache, w_uk, w_uv, d_out, sel, slot_blocks)
    ids = jnp.stack([lax.axis_index("seq"), lax.axis_index("grp")]).astype(jnp.int32)
    tokens = cache.shape[0]
    depth = width // groups
    lanes = per_peer * BLOCK_LEN
    held = peers // 2
    half = held * lanes
    share = heads // peers
    rows = heads * queries
    scale = 1.0 / math.sqrt(nope + rope)

    n_rows = w_uk.shape[1] // latent
    l_rows = w_uv.shape[1] // value
    tiles = latent // LANES
    uk = w_uk.reshape(heads, n_rows, tiles, LANES).transpose(0, 2, 1, 3)
    pack = jnp.concatenate(
        [
            uk.reshape(heads, n_rows * tiles, LANES),
            w_uv.reshape(heads, l_rows, value),
            q_nope.transpose(1, 0, 2),
            d_out.transpose(1, 0, 2),
        ],
        axis=1,
    )
    pack = seq_swap(pack).reshape(peers, share, -1, LANES)
    sizes = (n_rows * tiles, l_rows, queries, tiles, latent)
    (lat,) = call(
        functools.partial(expand_kernel, sizes),
        "expand",
        (pack,),
        [VMEM],
        [((peers, share, queries, 2 * latent), BF16)],
    )
    qd = seq_swap(lat).reshape(rows, 2 * latent)

    row1 = swap(slot_blocks, "seq", 1)
    (c0,) = call(
        cut_kernel, "cut", (ids, cache.T), [SMEM, VMEM], [((depth, tokens), BF16)]
    )
    c2 = swap(c0, "seq", 4)
    c1 = swap(c0, "seq", 2)
    c3 = swap(c2, "seq", 2)
    away, k0 = call(
        functools.partial(gather_kernel, per_peer),
        "gather",
        (ids, slot_blocks, row1, c0, c1, c2, c3),
        [SMEM] * 3 + [VMEM] * 4,
        [((depth, half), BF16)] * 2,
    )
    keys = []
    for k in (k0, swap(away, "seq", 1)):
        k2 = swap(k, "grp", 2)
        keys += [k, swap(k, "grp", 1), k2, swap(k2, "grp", 1)]
    asked = jnp.concatenate([slot_blocks, row1], axis=0)
    for bit in (2, 4):
        asked = jnp.concatenate([asked, swap(asked, "seq", bit)], axis=0)

    rope_rows = q_rope.transpose(1, 0, 2)
    kt, pb, cat, o_lat, delta, keep, send, dq = call(
        functools.partial(first_kernel, scale, per_peer),
        "first",
        (ids, sel, rope_rows, qd, *keys),
        [SMEM] + [VMEM] * 11,
        [
            ((width + slots, half), BF16),
            ((rows, half), BF16),
            ((width, 2 * rows), BF16),
            ((rows, latent), BF16),
            ((rows, 1), F32),
            ((2, depth, half), BF16),
            ((2, depth, half), BF16),
            ((rows, width), F32),
        ],
        [
            pltpu.VMEM((width + slots, half), BF16),
            pltpu.VMEM((rows, half), BF16),
            pltpu.VMEM((rows, width + slots), BF16),
            pltpu.VMEM((rows, latent), BF16),
            pltpu.VMEM((rows, 2 * half), F32),
            pltpu.VMEM((width, 2 * rows), BF16),
            pltpu.VMEM((rows, latent), F32),
        ],
        40,
    )

    def pair(keep, send, tied=None):
        outs = [((depth, half), BF16)] * 2
        return call(pair_kernel, "pair", (keep, swap(send, "grp", 1)), [VMEM] * 2, outs, tied=tied)

    def owner(a0, a2, tied=None):
        outs = [((depth, lanes), BF16)] * held
        return call(owner_kernel, "owner", (a0, swap(a2, "grp", 2)), [VMEM] * 2, outs, tied=tied)

    far = (keep, send)
    keep, send, lat, d_rope = call(
        functools.partial(second_kernel, scale),
        "second",
        (qd, cat, delta, kt, pb, o_lat, dq),
        [VMEM] * 7,
        [
            ((2, depth, half), BF16),
            ((2, depth, half), BF16),
            ((rows, 2 * latent), BF16),
            ((rows, rope), BF16),
        ],
        [pltpu.VMEM((rows, latent), BF16), pltpu.VMEM((rows, width), F32)],
        28,
    )
    lat, *far = pair(*far, tied=lat)
    near = pair(keep, send)
    far = owner(*far)
    lat = seq_swap(lat.reshape(peers, share, queries, 2 * latent))
    (res,) = call(
        functools.partial(reduce_kernel, sizes),
        "reduce",
        (pack, lat),
        [VMEM] * 2,
        [((peers, share, queries, value + nope), BF16)],
    )
    res, *near = owner(*near, tied=res)
    got = exchange([*near, *far])
    res = seq_swap(res).reshape(heads, queries, value + nope)

    (y0,) = call(
        functools.partial(scatter_kernel, peers),
        "scatter",
        (ids, asked, *got),
        [SMEM, SMEM] + [VMEM] * peers,
        [((depth, tokens), BF16)],
        [pltpu.VMEM((depth, tokens), F32)],
    )
    y2 = swap(y0, "grp", 2)
    y1 = swap(y0, "grp", 1)
    y3 = swap(y2, "grp", 1)
    (d_cache,) = call(
        assemble_kernel,
        "assemble",
        (ids, y0, y1, y2, y3),
        [SMEM] + [VMEM] * 4,
        [((width, tokens), F32)],
    )
    return (
        res[:, :, :value].transpose(1, 0, 2),
        res[:, :, value:].transpose(1, 0, 2),
        d_rope.reshape(heads, queries, rope).transpose(1, 0, 2),
        d_cache.T,
    )


def local_general(q_nope, q_rope, cache, w_uk, w_uv, d_out, sel, slot_blocks):
    peers = lax.axis_size("seq")
    queries, heads, nope = q_nope.shape
    rope = q_rope.shape[2]
    width = cache.shape[1]
    latent = width - rope
    value = d_out.shape[2]
    slot_total = slot_blocks.shape[1]
    per_peer = slot_total // peers
    own_blocks = cache.shape[0] // BLOCK_LEN
    scale = 1.0 / math.sqrt(nope + rope)
    gathered_k, gathered_v = (
        lax.all_gather(w_uk, "seq", axis=1, tiled=True),
        lax.all_gather(w_uv, "seq", axis=1, tiled=True),
    )
    weight_k = gathered_k.reshape(heads, nope, latent)
    weight_v = gathered_v.reshape(heads, latent, value)
    wanted = slot_blocks.reshape(peers, per_peer)
    asked = lax.all_to_all(wanted, "seq", split_axis=0, concat_axis=0, tiled=True)
    blocks = cache.reshape(own_blocks, BLOCK_LEN, width)
    arrived = lax.all_to_all(blocks[asked], "seq", split_axis=0, concat_axis=0, tiled=True)
    keys = arrived.reshape(slot_total * BLOCK_LEN, width)
    keys_lat = keys[:, :latent]
    q_lat = jnp.einsum("qhn,hnl->qhl", q_nope, weight_k, preferred_element_type=jnp.float32).astype(
        jnp.bfloat16
    )
    qfull = jnp.concatenate([q_lat, q_rope], axis=-1)
    chosen = jnp.any(
        sel[:, :, None] == jnp.arange(slot_total, dtype=jnp.int32)[None, None, :], axis=1
    )
    live = jnp.repeat(chosen, BLOCK_LEN, axis=1)[:, None, :]
    score = jnp.einsum("qhc,tc->qht", qfull, keys, preferred_element_type=jnp.float32) * scale
    score = jnp.where(live, score, -jnp.inf)
    prob = jax.nn.softmax(score, axis=-1)
    prob_low = prob.astype(jnp.bfloat16)
    olat = jnp.einsum("qht,tl->qhl", prob_low, keys_lat, preferred_element_type=jnp.float32).astype(
        jnp.bfloat16
    )
    attn_out = jnp.einsum(
        "qhl,hlv->qhv", olat, weight_v, preferred_element_type=jnp.float32
    ).astype(jnp.bfloat16)
    d_olat = jnp.einsum("qhv,hlv->qhl", d_out, weight_v, preferred_element_type=jnp.float32).astype(
        jnp.bfloat16
    )
    dprob = jnp.einsum("qhl,tl->qht", d_olat, keys_lat, preferred_element_type=jnp.float32)
    delta = jnp.sum(prob * dprob, axis=-1, keepdims=True)
    dscore = (prob * (dprob - delta) * scale).astype(jnp.bfloat16)
    dquery = jnp.einsum("qht,tc->qhc", dscore, keys, preferred_element_type=jnp.float32)
    d_q_rope = dquery[:, :, latent:].astype(jnp.bfloat16)
    d_qlat = dquery[:, :, :latent].astype(jnp.bfloat16)
    d_q_nope = jnp.einsum(
        "qhl,hnl->qhn", d_qlat, weight_k, preferred_element_type=jnp.float32
    ).astype(jnp.bfloat16)
    value_part = jnp.einsum("qht,qhl->tl", prob_low, d_olat, preferred_element_type=jnp.float32)
    dkeys = jnp.einsum("qht,qhc->tc", dscore, qfull, preferred_element_type=jnp.float32)
    dkeys = dkeys + jnp.pad(value_part, ((0, 0), (0, rope)))
    one_hot = (
        asked.reshape(-1)[:, None] == jnp.arange(own_blocks, dtype=jnp.int32)[None, :]
    ).astype(jnp.float32)
    returned = lax.all_to_all(
        dkeys.reshape(peers, per_peer, BLOCK_LEN * width).astype(jnp.bfloat16),
        "seq",
        split_axis=0,
        concat_axis=0,
        tiled=True,
    ).astype(jnp.float32)
    local_grad = jnp.dot(
        one_hot.T,
        returned.reshape(peers * per_peer, BLOCK_LEN * width),
        precision=lax.Precision.HIGHEST,
    )
    d_cache = (
        lax.psum(local_grad.astype(jnp.bfloat16), "grp")
        .astype(jnp.float32)
        .reshape(own_blocks * BLOCK_LEN, width)
    )
    return (attn_out, d_q_nope, d_q_rope, d_cache)


def solution(mesh):
    return jax.shard_map(
        local,
        mesh=mesh,
        in_specs=(
            P("seq", "grp", None),
            P("seq", "grp", None),
            P("seq", None),
            P("grp", "seq"),
            P("grp", "seq"),
            P("seq", "grp", None),
            P("seq", None),
            P("seq", None),
        ),
        out_specs=(
            P("seq", "grp", None),
            P("seq", "grp", None),
            P("seq", "grp", None),
            P("seq", None),
        ),
        check_vma=False,
    )
```

profile of v0, /device:TPU:0, one launch (start us, length us, event | category | flops | bytes accessed | tf_op | source)
XLA Modules:
  0.0 231.0 jit_solution(17740366130169896224)
XLA Ops:
  0.6 1.5 reshape.32
  3.1 1.1 pad_maximum_fusion
  4.3 7.3 %all-to-all-start = ((bf16[32,160,128]{2,1,0:T(8,128)(2,1)}), bf16[32,160,128]{2,1,0:T(8,128)(2,1)S(1)}, u32[]{:S(2)}, u32[]{:S(2)}) async-start(bf16[32,160,128]{2,1,0:T(8,128)(2,1)} %pad_maximum_fusion), calls=%async_computation | async-start | bytes 2621440 | tf_op jit(solution)/shard_map/all_to_all | solution.py:61
  11.6 1.3 copy-done.1
  13.5 3.0 %collective-permute-start.2 = (bf16[144,1024]{1,0:T(8,128)(2,1)S(1)}, bf16[144,1024]{1,0:T(8,128)(2,1)S(1)}, u32[]{:S(2)}, u32[]{:S(2)}) collective-permute-start(bf16[144,1024]{1,0:T(8,128)(2,1)S(1)} %cut.1.refs_0_), channel_id=1, source_target_pairs={{0,16},{4,20},{8,24},{12,28},{16,0},{20,4},{24,8},{28,12},{1,17},{... | collective-permute-start | bytes 884744 | tf_op jit(solution)/shard_map/ppermute | solution.py:57
  16.5 1.5 collective-permute-start.1
  17.9 37.7 %collective-permute-done.2.refs_2_ = bf16[144,1024]{1,0:T(8,128)(2,1)S(1)} collective-permute-done((bf16[144,1024]{1,0:T(8,128)(2,1)S(1)}, bf16[144,1024]{1,0:T(8,128)(2,1)S(1)}, u32[]{:S(2)}, u32[]{:S(2)}) %collective-permute-start.2) | collective-permute-done | bytes 294944 | tf_op jit(solution)/shard_map/ppermute | solution.py:57
  55.6 1.4 expand.1
  57.0 4.3 %all-to-all-start.1 = ((bf16[8,4,16,1024]{3,2,1,0:T(8,128)(2,1)}), bf16[8,4,16,1024]{3,2,1,0:T(8,128)(2,1)S(1)}, u32[]{:S(2)}, u32[]{:S(2)}) async-start(bf16[8,4,16,1024]{3,2,1,0:T(8,128)(2,1)} %expand.1), calls=%async_computation.1 | async-start | bytes 2097152 | tf_op jit(solution)/shard_map/all_to_all | solution.py:61
  61.3 2.0 collective-permute-start
  63.3 4.7 %collective-permute-done.other = s32[1,64]{1,0:T(1,128)S(1)} collective-permute-done((s32[1,64]{1,0:T(1,128)S(1)}, s32[1,64]{1,0:T(1,128)S(1)}, u32[]{:S(2)}, u32[]{:S(2)}) %collective-permute-start) | collective-permute-done | bytes 288 | tf_op jit(solution)/shard_map/ppermute | solution.py:57
  71.5 3.3 %gather.1 = (bf16[144,2048]{1,0:T(8,128)(2,1)S(1)}, bf16[144,2048]{1,0:T(8,128)(2,1)S(1)}) custom-call(s32[2]{0:T(128)S(1)} %pad_add_fusion.3.ids, s32[1,64]{1,0:T(1,128)S(1)} %copy-done.26, s32[1,64]{1,0:T(1,128)S(1)} %collective-permute-done.other, bf16[144,1024]{1,0:T(8,128)(2,1)S(1)} %cut.1.refs_0_, bf16[144,1024]{1,0:T(8,128)(2,1)S(1)} %copy-done.21, ...), custom_call_target="tpu_custom_call" | custom-call | tf_op jit(solution)/shard_map/gather/pallas_call | solution.py:35
  74.8 2.8 %collective-permute-start.7 = (bf16[144,2048]{1,0:T(8,128)(2,1)S(1)}, bf16[144,2048]{1,0:T(8,128)(2,1)S(1)}, u32[]{:S(2)}, u32[]{:S(2)}) collective-permute-start(bf16[144,2048]{1,0:T(8,128)(2,1)S(1)} %get-tuple-element.33), channel_id=1, source_target_pairs={{0,4},{4,0},{8,12},{12,8},{16,20},{20,16},{24,28},{28,24},{1,5},{5... | collective-permute-start | bytes 1769480 | tf_op jit(solution)/shard_map/ppermute | solution.py:57
  77.6 1.5 collective-permute-start.5
  79.1 11.3 %collective-permute-done.7.refs_4_ = bf16[144,2048]{1,0:T(8,128)(2,1)S(1)} collective-permute-done((bf16[144,2048]{1,0:T(8,128)(2,1)S(1)}, bf16[144,2048]{1,0:T(8,128)(2,1)S(1)}, u32[]{:S(2)}, u32[]{:S(2)}) %collective-permute-start.7) | collective-permute-done | bytes 589856 | tf_op jit(solution)/shard_map/ppermute | solution.py:57
  90.4 1.5 collective-permute-start.9
  94.1 8.8 %collective-permute-done.9.refs_6_ = bf16[144,2048]{1,0:T(8,128)(2,1)S(1)} collective-permute-done((bf16[144,2048]{1,0:T(8,128)(2,1)S(1)}, bf16[144,2048]{1,0:T(8,128)(2,1)S(1)}, u32[]{:S(2)}, u32[]{:S(2)}) %collective-permute-start.9) | collective-permute-done | bytes 589856 | tf_op jit(solution)/shard_map/ppermute | solution.py:57
  108.0 1.1 copy-done.3
  109.1 1.1 copy-done.5
  110.2 1.1 copy-done.7
  111.2 1.1 copy-done.9
  116.2 14.8 %first.1 = (bf16[640,2048]{1,0:T(8,128)(2,1)}, bf16[512,2048]{1,0:T(8,128)(2,1)S(1)}, bf16[576,1024]{1,0:T(8,128)(2,1)S(1)}, bf16[512,512]{1,0:T(8,128)(2,1)S(1)...) custom-call(s32[2]{0:T(128)S(1)} %pad_add_fusion.3.ids, ...), custom_call_target="tpu_custom_call" | custom-call | tf_op jit(solution)/shard_map/first/pallas_call | solution.py:35
  131.5 1.7 copy-done
  133.3 6.5 %second.1 = (bf16[2,144,2048]{2,1,0:T(8,128)(2,1)S(1)}, bf16[2,144,2048]{2,1,0:T(8,128)(2,1)S(1)}, bf16[512,1024]{1,0:T(8,128)(2,1)}, bf16[512,64]{1,0:T(8,128)(2,1)S(1)}) custom-call(bf16[512,1024]{1,0:T(8,128)(2,1)S(1)} %bitcast.28, bf16[576,1024]{1,0:T(8,128)(2,1)S(1)} %get-tuple-element.34.cat, f32[512,1]{1,0:T(8,128)S(1)} %get-tuple-element.35.delta, ...), custom_call_target="tpu_custom_call" | custom-call | tf_op jit(solution)/shard_map/second/pallas_call | solution.py:35
  143.1 12.5 %all-to-all-start.2 = ((bf16[8,4,16,1024]{3,2,1,0:T(8,128)(2,1)}), bf16[8,4,16,1024]{3,2,1,0:T(8,128)(2,1)S(1)}, u32[]{:S(2)}, u32[]{:S(2)}) async-start(bf16[8,4,16,1024]{3,2,1,0:T(8,128)(2,1)} %bitcast.10), calls=%async_computation.2 | async-start | bytes 2097152 | tf_op jit(solution)/shard_map/all_to_all | solution.py:61
  155.6 1.6 collective-permute-start.19
  157.2 1.5 collective-permute-done.12.got
  160.5 1.5 collective-permute-start.13
  162.0 10.0 %collective-permute-done.19.got = bf16[144,2048]{1,0:T(8,128)(2,1)S(1)} collective-permute-done((bf16[144,2048]{1,0:T(8,128)(2,1)}, bf16[144,2048]{1,0:T(8,128)(2,1)S(1)}, u32[]{:S(2)}, u32[]{:S(2)}) %collective-permute-start.19) | collective-permute-done | bytes 589856 | tf_op jit(solution)/shard_map/ppermute | solution.py:57
  174.2 2.9 %collective-permute-start.20 = (bf16[144,512]{1,0:T(8,128)(2,1)}, bf16[144,512]{1,0:T(8,128)(2,1)}, u32[]{:S(2)}, u32[]{:S(2)}) collective-permute-start(bf16[144,512]{1,0:T(8,128)(2,1)} %get-tuple-element.56), channel_id=1, source_target_pairs={{0,16},{4,20},{8,24},{12,28},{16,0},{20,4},{24,8},{28,12},{1,17},{... | collective-permute-start | bytes 442376 | tf_op jit(solution)/shard_map/ppermute | solution.py:57
  177.0 1.5 collective-permute-start.21
  179.0 1.5 collective-permute-start.14
  180.5 8.5 %all-to-all-done.2.lat = bf16[8,4,16,1024]{3,2,1,0:T(8,128)(2,1)S(1)} async-done(((bf16[8,4,16,1024]{3,2,1,0:T(8,128)(2,1)}), bf16[8,4,16,1024]{3,2,1,0:T(8,128)(2,1)S(1)}, u32[]{:S(2)}, u32[]{:S(2)}) %all-to-all-start.2) | async-done | bytes 1048608 | tf_op jit(solution)/shard_map/all_to_all | solution.py:61
  189.0 1.2 reduce.1.refs_0_
  190.4 3.6 %all-to-all-start.3 = ((bf16[8,4,16,256]{3,2,1,0:T(8,128)(2,1)}), bf16[8,4,16,256]{3,2,1,0:T(8,128)(2,1)S(1)}, u32[]{:S(2)}, u32[]{:S(2)}) async-start(bf16[8,4,16,256]{3,2,1,0:T(8,128)(2,1)} %get-tuple-element.48), calls=%async_computation.3 | async-start | bytes 524288 | tf_op jit(solution)/shard_map/all_to_all | solution.py:61
  194.0 2.9 %collective-permute-start.15 = (s32[4,64]{1,0:T(4,128)S(1)}, s32[4,64]{1,0:T(4,128)S(1)}, u32[]{:S(2)}, u32[]{:S(2)}) collective-permute-start(s32[4,64]{1,0:T(4,128)S(1)} %pad_add_fusion.1), channel_id=1, source_target_pairs={{0,16},{4,20},{8,24},{12,28},{16,0},{20,4},{24,8},{28,12},{1,17},{... | collective-permute-start | bytes 3080 | tf_op jit(solution)/shard_map/ppermute | solution.py:57
  196.9 1.4 collective-permute-start.22
  198.3 3.3 %collective-permute-start.23 = (bf16[144,512]{1,0:T(8,128)(2,1)S(1)}, bf16[144,512]{1,0:T(8,128)(2,1)S(1)}, u32[]{:S(2)}, u32[]{:S(2)}) collective-permute-start(bf16[144,512]{1,0:T(8,128)(2,1)S(1)} %copy-done.31), channel_id=1, source_target_pairs={{0,28},{4,24},{8,20},{12,16},{16,12},{20,8},{24,4},{28,0},{1,29},{... | collective-permute-start | bytes 442376 | tf_op jit(solution)/shard_map/ppermute | solution.py:57
  201.6 8.4 %collective-permute-done.15 = s32[4,64]{1,0:T(4,128)S(1)} collective-permute-done((s32[4,64]{1,0:T(4,128)S(1)}, s32[4,64]{1,0:T(4,128)S(1)}, u32[]{:S(2)}, u32[]{:S(2)}) %collective-permute-start.15) | collective-permute-done | bytes 1056 | tf_op jit(solution)/shard_map/ppermute | solution.py:57
  210.0 1.2 collective-permute-start.16
  211.2 2.2 collective-permute-start.18
  213.5 1.6 collective-permute-done.16.refs_1_
  215.1 1.2 collective-permute-done.17.refs_2_
  216.4 1.8 collective-permute-done.18.refs_3_
  218.2 2.3 %scatter.1.refs_0_ = bf16[144,1024]{1,0:T(8,128)(2,1)S(1)} custom-call(s32[2]{0:T(128)S(1)} %pad_add_fusion.3.ids, s32[8,64]{1,0:T(8,128)S(1)} %pad_add_fusion.rows, bf16[144,512]{1,0:T(8,128)(2,1)S(1)} %get-tuple-element.50.refs_0_, bf16[144,512]{1,0:T(8,128)(2,1)S(1)} %collective-permute-done.16.refs_1_, ...), custom_call_target="tpu_custom_call" | custom-call | tf_op jit(solution)/shard_map/scatter/pallas_call | solution.py:35
  220.5 1.6 collective-permute-start.25
  222.8 4.5 %collective-permute-done.25.refs_2_ = bf16[144,1024]{1,0:T(8,128)(2,1)S(1)} collective-permute-done((bf16[144,1024]{1,0:T(8,128)(2,1)S(1)}, bf16[144,1024]{1,0:T(8,128)(2,1)S(1)}, u32[]{:S(2)}, u32[]{:S(2)}) %collective-permute-start.25) | collective-permute-done | bytes 294944 | tf_op jit(solution)/shard_map/ppermute | solution.py:57
  228.9 2.1 assemble.1
  (114 shorter events, 27.0 us)
Async XLA Ops:
  0.6 1.6 copy-start.34
  4.3 51.3 %all-to-all-start = ((bf16[32,160,128]{2,1,0:T(8,128)(2,1)}), bf16[32,160,128]{2,1,0:T(8,128)(2,1)S(1)}, u32[]{:S(2)}, u32[]{:S(2)}) async-start(bf16[32,160,128]{2,1,0:T(8,128)(2,1)} %pad_maximum_fusion), calls=%async_computation | async-start | bytes 2621440 | tf_op jit(solution)/shard_map/all_to_all | solution.py:61
  11.6 1.3 copy-start.1
  13.5 42.1 %collective-permute-start.2 = (bf16[144,1024]{1,0:T(8,128)(2,1)S(1)}, bf16[144,1024]{1,0:T(8,128)(2,1)S(1)}, u32[]{:S(2)}, u32[]{:S(2)}) collective-permute-start(bf16[144,1024]{1,0:T(8,128)(2,1)S(1)} %cut.1.refs_0_), channel_id=1, source_target_pairs={{0,16},{4,20},{8,24},{12,28},{16,0},{20,4},{24,8},{28,12},{1,17},{... | collective-permute-start | bytes 884744 | tf_op jit(solution)/shard_map/ppermute | solution.py:57
  16.5 51.6 %collective-permute-start.1 = (bf16[144,1024]{1,0:T(8,128)(2,1)S(1)}, bf16[144,1024]{1,0:T(8,128)(2,1)S(1)}, u32[]{:S(2)}, u32[]{:S(2)}) collective-permute-start(bf16[144,1024]{1,0:T(8,128)(2,1)S(1)} %cut.1.refs_0_), channel_id=1, source_target_pairs={{0,8},{4,12},{8,0},{12,4},{16,24},{20,28},{24,16},{28,20},{1,9},{5... | collective-permute-start | bytes 884744 | tf_op jit(solution)/shard_map/ppermute | solution.py:57
  55.6 13.2 %collective-permute-start.3 = (bf16[144,1024]{1,0:T(8,128)(2,1)S(1)}, bf16[144,1024]{1,0:T(8,128)(2,1)S(1)}, u32[]{:S(2)}, u32[]{:S(2)}) collective-permute-start(bf16[144,1024]{1,0:T(8,128)(2,1)S(1)} %collective-permute-done.2.refs_2_), channel_id=1, source_target_pairs={{0,8},{4,12},{8,0},{12,4},{16,24},{20,28},{24,16},{28,20},{1,9},{5... | collective-permute-start | bytes 884744 | tf_op jit(solution)/shard_map/ppermute | solution.py:57
  57.0 4.3 %copy-start.26 = (s32[1,64]{1,0:T(1,128)S(1)}, s32[1,64]{1,0:T(1,128)}, u32[]{:S(2)}) copy-start(s32[1,64]{1,0:T(1,128)} %own.1) | copy-start | bytes 772
  57.0 51.0 %all-to-all-start.1 = ((bf16[8,4,16,1024]{3,2,1,0:T(8,128)(2,1)}), bf16[8,4,16,1024]{3,2,1,0:T(8,128)(2,1)S(1)}, u32[]{:S(2)}, u32[]{:S(2)}) async-start(bf16[8,4,16,1024]{3,2,1,0:T(8,128)(2,1)} %expand.1), calls=%async_computation.1 | async-start | bytes 2097152 | tf_op jit(solution)/shard_map/all_to_all | solution.py:61
  61.3 6.8 %collective-permute-start = (s32[1,64]{1,0:T(1,128)S(1)}, s32[1,64]{1,0:T(1,128)S(1)}, u32[]{:S(2)}, u32[]{:S(2)}) collective-permute-start(s32[1,64]{1,0:T(1,128)S(1)} %copy-done.26), channel_id=1, source_target_pairs={{0,4},{4,0},{8,12},{12,8},{16,20},{20,16},{24,28},{28,24},{1,5},{5... | collective-permute-start | bytes 776 | tf_op jit(solution)/shard_map/ppermute | solution.py:57
  74.8 15.6 %collective-permute-start.7 = (bf16[144,2048]{1,0:T(8,128)(2,1)S(1)}, bf16[144,2048]{1,0:T(8,128)(2,1)S(1)}, u32[]{:S(2)}, u32[]{:S(2)}) collective-permute-start(bf16[144,2048]{1,0:T(8,128)(2,1)S(1)} %get-tuple-element.33), channel_id=1, source_target_pairs={{0,4},{4,0},{8,12},{12,8},{16,20},{20,16},{24,28},{28,24},{1,5},{5... | collective-permute-start | bytes 1769480 | tf_op jit(solution)/shard_map/ppermute | solution.py:57
  77.6 15.6 %collective-permute-start.5 = (bf16[144,2048]{1,0:T(8,128)(2,1)S(1)}, bf16[144,2048]{1,0:T(8,128)(2,1)S(1)}, u32[]{:S(2)}, u32[]{:S(2)}) collective-permute-start(bf16[144,2048]{1,0:T(8,128)(2,1)S(1)} %get-tuple-element.32.refs_0_), channel_id=1, source_target_pairs={{0,2},{1,3},{2,0},{3,1},{4,6},{5,7},{6,4},{7,5},{8,10},{9,11},{10,... | collective-permute-start | bytes 1769480 | tf_op jit(solution)/shard_map/ppermute | solution.py:57
  90.4 12.5 %collective-permute-start.9 = (bf16[144,2048]{1,0:T(8,128)(2,1)S(1)}, bf16[144,2048]{1,0:T(8,128)(2,1)S(1)}, u32[]{:S(2)}, u32[]{:S(2)}) collective-permute-start(bf16[144,2048]{1,0:T(8,128)(2,1)S(1)} %collective-permute-done.7.refs_4_), channel_id=1, source_target_pairs={{0,2},{1,3},{2,0},{3,1},{4,6},{5,7},{6,4},{7,5},{8,10},{9,11},{10,... | collective-permute-start | bytes 1769480 | tf_op jit(solution)/shard_map/ppermute | solution.py:57
  91.9 12.8 %collective-permute-start.4 = (bf16[144,2048]{1,0:T(8,128)(2,1)S(1)}, bf16[144,2048]{1,0:T(8,128)(2,1)S(1)}, u32[]{:S(2)}, u32[]{:S(2)}) collective-permute-start(bf16[144,2048]{1,0:T(8,128)(2,1)S(1)} %get-tuple-element.32.refs_0_), channel_id=1, source_target_pairs={{0,1},{1,0},{2,3},{3,2},{4,5},{5,4},{6,7},{7,6},{8,9},{9,8},{10,11... | collective-permute-start | bytes 1769480 | tf_op jit(solution)/shard_map/ppermute | solution.py:57
  91.9 14.4 %collective-permute-start.8 = (bf16[144,2048]{1,0:T(8,128)(2,1)S(1)}, bf16[144,2048]{1,0:T(8,128)(2,1)S(1)}, u32[]{:S(2)}, u32[]{:S(2)}) collective-permute-start(bf16[144,2048]{1,0:T(8,128)(2,1)S(1)} %collective-permute-done.7.refs_4_), channel_id=1, source_target_pairs={{0,1},{1,0},{2,3},{3,2},{4,5},{5,4},{6,7},{7,6},{8,9},{9,8},{10,11... | collective-permute-start | bytes 1769480 | tf_op jit(solution)/shard_map/ppermute | solution.py:57
  93.3 12.3 %collective-permute-start.6 = (bf16[144,2048]{1,0:T(8,128)(2,1)S(1)}, bf16[144,2048]{1,0:T(8,128)(2,1)S(1)}, u32[]{:S(2)}, u32[]{:S(2)}) collective-permute-start(bf16[144,2048]{1,0:T(8,128)(2,1)S(1)} %collective-permute-done.5.refs_2_), channel_id=1, source_target_pairs={{0,1},{1,0},{2,3},{3,2},{4,5},{5,4},{6,7},{7,6},{8,9},{9,8},{10,11... | collective-permute-start | bytes 1769480 | tf_op jit(solution)/shard_map/ppermute | solution.py:57
  102.9 4.3 %collective-permute-start.10 = (bf16[144,2048]{1,0:T(8,128)(2,1)S(1)}, bf16[144,2048]{1,0:T(8,128)(2,1)S(1)}, u32[]{:S(2)}, u32[]{:S(2)}) collective-permute-start(bf16[144,2048]{1,0:T(8,128)(2,1)S(1)} %collective-permute-done.9.refs_6_), channel_id=1, source_target_pairs={{0,1},{1,0},{2,3},{3,2},{4,5},{5,4},{6,7},{7,6},{8,9},{9,8},{10,11... | collective-permute-start | bytes 1769480 | tf_op jit(solution)/shard_map/ppermute | solution.py:57
  108.0 1.1 copy-start.3
  109.1 1.1 copy-start.5
  110.2 1.1 copy-start.7
  111.2 1.1 copy-start.9
  112.3 1.1 copy-start.11
  113.4 1.1 copy-start.13
  114.4 1.1 copy-start.15
  131.0 9.8 %collective-permute-start.11 = (bf16[2,144,2048]{2,1,0:T(8,128)(2,1)S(1)}, bf16[2,144,2048]{2,1,0:T(8,128)(2,1)S(1)}, u32[]{:S(2)}, u32[]{:S(2)}) collective-permute-start(bf16[2,144,2048]{2,1,0:T(8,128)(2,1)S(1)} %get-tuple-element.42), channel_id=1, source_target_pairs={{0,1},{1,0},{2,3},{3,2},{4,5},{5,4},{6,7},{7,6},{8,9},{9,8},{10,11... | collective-permute-start | bytes 3538952 | tf_op jit(solution)/shard_map/ppermute | solution.py:57
  131.5 1.7 copy-start
  139.8 1.0 copy-start.28
  143.1 46.0 %all-to-all-start.2 = ((bf16[8,4,16,1024]{3,2,1,0:T(8,128)(2,1)}), bf16[8,4,16,1024]{3,2,1,0:T(8,128)(2,1)S(1)}, u32[]{:S(2)}, u32[]{:S(2)}) async-start(bf16[8,4,16,1024]{3,2,1,0:T(8,128)(2,1)} %bitcast.10), calls=%async_computation.2 | async-start | bytes 2097152 | tf_op jit(solution)/shard_map/all_to_all | solution.py:61
  155.6 16.5 %copy-start.19 = (bf16[144,2048]{1,0:T(8,128)(2,1)S(1)}, bf16[144,2048]{1,0:T(8,128)(2,1)}, u32[]{:S(2)}) copy-start(bf16[144,2048]{1,0:T(8,128)(2,1)} %copy-done.18) | copy-start | bytes 1769476
  155.6 3.1 %collective-permute-start.12 = (bf16[2,144,2048]{2,1,0:T(8,128)(2,1)}, bf16[2,144,2048]{2,1,0:T(8,128)(2,1)S(1)}, u32[]{:S(2)}, u32[]{:S(2)}) collective-permute-start(bf16[2,144,2048]{2,1,0:T(8,128)(2,1)} %copy-done.28), channel_id=1, source_target_pairs={{0,1},{1,0},{2,3},{3,2},{4,5},{5,4},{6,7},{7,6},{8,9},{9,8},{10,11... | collective-permute-start | bytes 3538952 | tf_op jit(solution)/shard_map/ppermute | solution.py:57
  155.6 16.4 %collective-permute-start.19 = (bf16[144,2048]{1,0:T(8,128)(2,1)}, bf16[144,2048]{1,0:T(8,128)(2,1)S(1)}, u32[]{:S(2)}, u32[]{:S(2)}) collective-permute-start(bf16[144,2048]{1,0:T(8,128)(2,1)} %copy-done.29), channel_id=1, source_target_pairs={{0,2},{1,3},{2,0},{3,1},{4,6},{5,7},{6,4},{7,5},{8,10},{9,11},{10,... | collective-permute-start | bytes 1769480 | tf_op jit(solution)/shard_map/ppermute | solution.py:57
  160.5 29.7 %collective-permute-start.13 = (bf16[144,2048]{1,0:T(8,128)(2,1)}, bf16[144,2048]{1,0:T(8,128)(2,1)S(1)}, u32[]{:S(2)}, u32[]{:S(2)}) collective-permute-start(bf16[144,2048]{1,0:T(8,128)(2,1)} %get-tuple-element.47), channel_id=1, source_target_pairs={{0,2},{1,3},{2,0},{3,1},{4,6},{5,7},{6,4},{7,5},{8,10},{9,11},{10,... | collective-permute-start | bytes 1769480 | tf_op jit(solution)/shard_map/ppermute | solution.py:57
  174.2 37.1 %collective-permute-start.20 = (bf16[144,512]{1,0:T(8,128)(2,1)}, bf16[144,512]{1,0:T(8,128)(2,1)}, u32[]{:S(2)}, u32[]{:S(2)}) collective-permute-start(bf16[144,512]{1,0:T(8,128)(2,1)} %get-tuple-element.56), channel_id=1, source_target_pairs={{0,16},{4,20},{8,24},{12,28},{16,0},{20,4},{24,8},{28,12},{1,17},{... | collective-permute-start | bytes 442376 | tf_op jit(solution)/shard_map/ppermute | solution.py:57
  177.0 34.2 %collective-permute-start.21 = (bf16[144,512]{1,0:T(8,128)(2,1)}, bf16[144,512]{1,0:T(8,128)(2,1)}, u32[]{:S(2)}, u32[]{:S(2)}) collective-permute-start(bf16[144,512]{1,0:T(8,128)(2,1)} %get-tuple-element.57), channel_id=1, source_target_pairs={{0,20},{4,16},{8,28},{12,24},{16,4},{20,0},{24,12},{28,8},{1,21},{... | collective-permute-start | bytes 442376 | tf_op jit(solution)/shard_map/ppermute | solution.py:57
  179.0 11.2 %copy-start.17 = (bf16[144,2048]{1,0:T(8,128)(2,1)S(1)}, bf16[144,2048]{1,0:T(8,128)(2,1)}, u32[]{:S(2)}) copy-start(bf16[144,2048]{1,0:T(8,128)(2,1)} %copy-done.16) | copy-start | bytes 1769476
  179.0 14.9 %collective-permute-start.14 = (s32[2,64]{1,0:T(2,128)}, s32[2,64]{1,0:T(2,128)S(1)}, u32[]{:S(2)}, u32[]{:S(2)}) collective-permute-start(s32[2,64]{1,0:T(2,128)} %pad_add_fusion.2), channel_id=1, source_target_pairs={{0,8},{4,12},{8,0},{12,4},{16,24},{20,28},{24,16},{28,20},{1,9},{5... | collective-permute-start | bytes 1544 | tf_op jit(solution)/shard_map/ppermute | solution.py:57
  190.2 6.7 %copy-start.33 = (bf16[144,512]{1,0:T(8,128)(2,1)S(1)}, bf16[144,512]{1,0:T(8,128)(2,1)}, u32[]{:S(2)}) copy-start(bf16[144,512]{1,0:T(8,128)(2,1)} %copy-done.32) | copy-start | bytes 442372
  190.2 8.1 %copy-start.31 = (bf16[144,512]{1,0:T(8,128)(2,1)S(1)}, bf16[144,512]{1,0:T(8,128)(2,1)}, u32[]{:S(2)}) copy-start(bf16[144,512]{1,0:T(8,128)(2,1)} %copy-done.30) | copy-start | bytes 442372
  190.4 31.7 %copy-start.25 = (bf16[512,64]{1,0:T(8,128)(2,1)S(1)}, bf16[512,64]{1,0:T(8,128)(2,1)}, u32[]{:S(2)}) copy-start(bf16[512,64]{1,0:T(8,128)(2,1)} %copy-done.24) | copy-start | bytes 196612
  190.4 37.0 %all-to-all-start.3 = ((bf16[8,4,16,256]{3,2,1,0:T(8,128)(2,1)}), bf16[8,4,16,256]{3,2,1,0:T(8,128)(2,1)S(1)}, u32[]{:S(2)}, u32[]{:S(2)}) async-start(bf16[8,4,16,256]{3,2,1,0:T(8,128)(2,1)} %get-tuple-element.48), calls=%async_computation.3 | async-start | bytes 524288 | tf_op jit(solution)/shard_map/all_to_all | solution.py:61
  194.0 16.0 %collective-permute-start.15 = (s32[4,64]{1,0:T(4,128)S(1)}, s32[4,64]{1,0:T(4,128)S(1)}, u32[]{:S(2)}, u32[]{:S(2)}) collective-permute-start(s32[4,64]{1,0:T(4,128)S(1)} %pad_add_fusion.1), channel_id=1, source_target_pairs={{0,16},{4,20},{8,24},{12,28},{16,0},{20,4},{24,8},{28,12},{1,17},{... | collective-permute-start | bytes 3080 | tf_op jit(solution)/shard_map/ppermute | solution.py:57
  196.9 16.6 %collective-permute-start.22 = (bf16[144,512]{1,0:T(8,128)(2,1)S(1)}, bf16[144,512]{1,0:T(8,128)(2,1)S(1)}, u32[]{:S(2)}, u32[]{:S(2)}) collective-permute-start(bf16[144,512]{1,0:T(8,128)(2,1)S(1)} %copy-done.33), channel_id=1, source_target_pairs={{0,24},{4,28},{8,16},{12,20},{16,8},{20,12},{24,0},{28,4},{1,25},{... | collective-permute-start | bytes 442376 | tf_op jit(solution)/shard_map/ppermute | solution.py:57
  198.3 15.2 %collective-permute-start.23 = (bf16[144,512]{1,0:T(8,128)(2,1)S(1)}, bf16[144,512]{1,0:T(8,128)(2,1)S(1)}, u32[]{:S(2)}, u32[]{:S(2)}) collective-permute-start(bf16[144,512]{1,0:T(8,128)(2,1)S(1)} %copy-done.31), channel_id=1, source_target_pairs={{0,28},{4,24},{8,20},{12,16},{16,12},{20,8},{24,4},{28,0},{1,29},{... | collective-permute-start | bytes 442376 | tf_op jit(solution)/shard_map/ppermute | solution.py:57
  210.0 5.1 %collective-permute-start.16 = (bf16[144,512]{1,0:T(8,128)(2,1)S(1)}, bf16[144,512]{1,0:T(8,128)(2,1)S(1)}, u32[]{:S(2)}, u32[]{:S(2)}) collective-permute-start(bf16[144,512]{1,0:T(8,128)(2,1)S(1)} %get-tuple-element.51), channel_id=1, source_target_pairs={{0,4},{4,0},{8,12},{12,8},{16,20},{20,16},{24,28},{28,24},{1,5},{5... | collective-permute-start | bytes 442376 | tf_op jit(solution)/shard_map/ppermute | solution.py:57
  211.2 5.1 %collective-permute-start.17 = (bf16[144,512]{1,0:T(8,128)(2,1)S(1)}, bf16[144,512]{1,0:T(8,128)(2,1)S(1)}, u32[]{:S(2)}, u32[]{:S(2)}) collective-permute-start(bf16[144,512]{1,0:T(8,128)(2,1)S(1)} %get-tuple-element.52), channel_id=1, source_target_pairs={{0,8},{4,12},{8,0},{12,4},{16,24},{20,28},{24,16},{28,20},{1,9},{5... | collective-permute-start | bytes 442376 | tf_op jit(solution)/shard_map/ppermute | solution.py:57
  211.2 6.9 %collective-permute-start.18 = (bf16[144,512]{1,0:T(8,128)(2,1)S(1)}, bf16[144,512]{1,0:T(8,128)(2,1)S(1)}, u32[]{:S(2)}, u32[]{:S(2)}) collective-permute-start(bf16[144,512]{1,0:T(8,128)(2,1)S(1)} %get-tuple-element.53), channel_id=1, source_target_pairs={{0,12},{4,8},{8,4},{12,0},{16,28},{20,24},{24,20},{28,16},{1,13},{... | collective-permute-start | bytes 442376 | tf_op jit(solution)/shard_map/ppermute | solution.py:57
  220.5 6.8 %collective-permute-start.25 = (bf16[144,1024]{1,0:T(8,128)(2,1)S(1)}, bf16[144,1024]{1,0:T(8,128)(2,1)S(1)}, u32[]{:S(2)}, u32[]{:S(2)}) collective-permute-start(bf16[144,1024]{1,0:T(8,128)(2,1)S(1)} %scatter.1.refs_0_), channel_id=1, source_target_pairs={{0,2},{1,3},{2,0},{3,1},{4,6},{5,7},{6,4},{7,5},{8,10},{9,11},{10,... | collective-permute-start | bytes 884744 | tf_op jit(solution)/shard_map/ppermute | solution.py:57
  222.8 5.4 %collective-permute-start.24 = (bf16[144,1024]{1,0:T(8,128)(2,1)S(1)}, bf16[144,1024]{1,0:T(8,128)(2,1)S(1)}, u32[]{:S(2)}, u32[]{:S(2)}) collective-permute-start(bf16[144,1024]{1,0:T(8,128)(2,1)S(1)} %scatter.1.refs_0_), channel_id=1, source_target_pairs={{0,1},{1,0},{2,3},{3,2},{4,5},{5,4},{6,7},{7,6},{8,9},{9,8},{10,11... | collective-permute-start | bytes 884744 | tf_op jit(solution)/shard_map/ppermute | solution.py:57
  227.3 1.6 collective-permute-start.26
  (20 other events, 16.1 us)
where the time goes:
time: 232 us; the launch traced here: 231 us
  waiting for transfers between devices  101 us (44%)
  starting transfers between devices  62.6 us (27%)
  Pallas kernels  34.4 us (15%)
  local copies, waits for them, and re-layouts  30.4 us (13%)
    ppermute x27, waiting for transfers between devices, swap(): return lax.ppermute(x, axis, [(i, i ^ bit) for i in range(n)])  92.4 us
    ppermute x27, starting transfers between devices, swap(): return lax.ppermute(x, axis, [(i, i ^ bit) for i in range(n)])  34.9 us
    pallas_call x12, Pallas kernels, call(): pl.pallas_call(body, out_shape=out_shape, in_specs=specs, out_specs=out_s...  34.4 us
    all_to_all x4, starting transfers between devices, seq_swap(): return lax.all_to_all(x, 'seq', split_axis=0, concat_axis=0, tiled=True)  27.6 us
    unnamed x76, local copies, waits for them, and re-layouts  27.2 us
    all_to_all x4, waiting for transfers between devices, seq_swap(): return lax.all_to_all(x, 'seq', split_axis=0, concat_axis=0, tiled=True)  8.55 us
  transfers between devices with their start and end apart: 31, of which 13 were waited for; matrix products, arithmetic and copies ran while one was open for 1% of the time, Pallas kernels for 7%

commit v1 on v0

--- a/solution.py
+++ b/solution.py
@@ -18,7 +18,7 @@
 BF16 = jnp.bfloat16
 
 
-def call(kernel, name, args, specs, outs, scratch=(), mib=32, tied=None):
+def call(kernel, name, args, specs, outs, scratch=(), tied=None):
     out_shape = [jax.ShapeDtypeStruct(s, d) for s, d in outs]
     out_specs = [VMEM] * len(outs)
     aliases = {}
@@ -39,7 +39,7 @@
         out_specs=out_specs,
         scratch_shapes=list(scratch),
         input_output_aliases=aliases,
-        compiler_params=pltpu.CompilerParams(vmem_limit_bytes=mib * 2**20),
+        compiler_params=pltpu.CompilerParams(vmem_limit_bytes=60 * 2**20),
         name=name,
     )(*args)
 
@@ -63,6 +63,10 @@
 
 def exchange(pieces):
     return [pieces[0]] + [swap(p, "seq", k) for k, p in enumerate(pieces) if k > 0]
+
+
+def copy_kernel(x, out):
+    out[...] = x[...]
 
 
 def cut_kernel(ids, cache, out):
@@ -160,7 +164,7 @@
             out[r, h, :, attn.shape[1] :] = dqn[r * queries : (r + 1) * queries]
 
 
-def far_or_near(grads, scale, do, cat, delta, kt, p, width):
+def tokens_grad(grads, scale, do, cat, delta, kt, p, width):
     keep, send, at, depth = grads
     latent = do.shape[1]
     dp = nn(do[...], kt[:latent])
@@ -172,10 +176,10 @@
     return part
 
 
-def first_kernel(scale, per_peer, ids, sel, rope, qd, *refs):
-    keys, refs = (refs[:4], refs[4:8]), refs[8:]
-    kt_near, pb_near, cat, o_lat, delta_out, keep, send, dq, refs = (*refs[:8], refs[8:])
-    kt_far, pb_far, qx, do, sc, flip, o_full = refs
+def attend_kernel(scale, per_peer, ids, sel, rope, qd, *refs):
+    keys, refs = (refs[:4], refs[4:8]), refs[9:]
+    keeps, sends, lat, d_rope, refs = (refs[0], refs[2]), (refs[1], refs[3]), refs[4], refs[5], refs[6:]
+    kt_near, kt_far, pb_near, pb_far, qx, do, sc, flip, cat, o_full, dq = refs
     rows, latent = do.shape
     heads, queries, rope_dim = rope.shape
     width = latent + rope_dim
@@ -228,9 +232,8 @@
             o_full[...] = part
         else:
             o_full[...] += part
-    o_lat[...] = o_full[...].astype(BF16)
+    lat[:, :latent] = o_full[...].astype(BF16)
     delta = jnp.sum(o_full[...] * do[...].astype(F32), axis=1, keepdims=True)
-    delta_out[...] = delta
 
     flip[:, :rows] = qx[:, :width].T
     flip[:latent, rows:] = do[...].T
@@ -238,30 +241,15 @@
     for k in range(4):
         at = pl.ds(pl.multiple_of((ids[1] ^ k) * depth, 16), depth)
         cat[k * depth : (k + 1) * depth] = flip[at, :]
-    for i in range(0, half, step):
+    for n, (c, i) in enumerate([(c, i) for c in (1, 0) for i in range(0, half, step)]):
         at = slice(i, i + step)
-        grads = (keep, send, at, depth)
-        part = far_or_near(grads, scale, do, cat, delta, kt_far.at[:, at], pb_far[:, at], width)
-        if i == 0:
+        grads = (keeps[c], sends[c], at, depth)
+        kt = kts[c].at[:, at]
+        part = tokens_grad(grads, scale, do, cat, delta, kt, pbs[c][:, at], width)
+        if n == 0:
             dq[...] = part
         else:
             dq[...] += part
-
-
-def second_kernel(scale, qd, cat, delta, kt, pb, o_lat, before, keep, send, lat, d_rope, do, dq):
-    rows, latent = do.shape
-    width = cat.shape[0]
-    depth = width // 4
-    do[...] = qd[:, latent:]
-    step = 512
-    dq[...] = before[...]
-    for i in range(0, pb.shape[1], step):
-        at = slice(i, i + step)
-        grads = (keep, send, at, depth)
-        dq[...] += far_or_near(
-            grads, scale, do, cat, delta[...], kt.at[:, at], pb[:, at], width
-        )
-    lat[:, :latent] = o_lat[...]
     lat[:, latent:] = dq[:, :latent].astype(BF16)
     d_rope[...] = dq[:, latent:].astype(BF16)
 
@@ -303,6 +291,9 @@
     rows = heads * queries
     scale = 1.0 / math.sqrt(nope + rope)
 
+    row1 = swap(slot_blocks, "seq", 1)
+    (c0,) = call(cut_kernel, "cut", (ids, cache.T), [SMEM, VMEM], [((depth, tokens), BF16)])
+
     n_rows = w_uk.shape[1] // latent
     l_rows = w_uv.shape[1] // value
     tiles = latent // LANES
@@ -316,6 +307,9 @@
         ],
         axis=1,
     )
+    pack, row1 = call(
+        copy_kernel, "after", (row1,), [VMEM], [(row1.shape, jnp.int32)], tied=pack
+    )
     pack = seq_swap(pack).reshape(peers, share, -1, LANES)
     sizes = (n_rows * tiles, l_rows, queries, tiles, latent)
     (lat,) = call(
@@ -327,10 +321,6 @@
     )
     qd = seq_swap(lat).reshape(rows, 2 * latent)
 
-    row1 = swap(slot_blocks, "seq", 1)
-    (c0,) = call(
-        cut_kernel, "cut", (ids, cache.T), [SMEM, VMEM], [((depth, tokens), BF16)]
-    )
     c2 = swap(c0, "seq", 4)
     c1 = swap(c0, "seq", 2)
     c3 = swap(c2, "seq", 2)
@@ -350,31 +340,23 @@
         asked = jnp.concatenate([asked, swap(asked, "seq", bit)], axis=0)
 
     rope_rows = q_rope.transpose(1, 0, 2)
-    kt, pb, cat, o_lat, delta, keep, send, dq = call(
-        functools.partial(first_kernel, scale, per_peer),
-        "first",
-        (ids, sel, rope_rows, qd, *keys),
-        [SMEM] + [VMEM] * 11,
-        [
-            ((width + slots, half), BF16),
-            ((rows, half), BF16),
-            ((width, 2 * rows), BF16),
-            ((rows, latent), BF16),
-            ((rows, 1), F32),
-            ((2, depth, half), BF16),
-            ((2, depth, half), BF16),
-            ((rows, width), F32),
-        ],
-        [
-            pltpu.VMEM((width + slots, half), BF16),
-            pltpu.VMEM((rows, half), BF16),
+    near_keep, near_send, far_keep, far_send, lat, d_rope = call(
+        functools.partial(attend_kernel, scale, per_peer),
+        "attend",
+        (ids, sel, rope_rows, qd, *keys, asked),
+        [SMEM] + [VMEM] * 11 + [ANY],
+        [((2, depth, half), BF16)] * 4 + [((rows, 2 * latent), BF16), ((rows, rope), BF16)],
+        [pltpu.VMEM((width + slots, half), BF16)] * 2
+        + [pltpu.VMEM((rows, half), BF16)] * 2
+        + [
             pltpu.VMEM((rows, width + slots), BF16),
             pltpu.VMEM((rows, latent), BF16),
             pltpu.VMEM((rows, 2 * half), F32),
             pltpu.VMEM((width, 2 * rows), BF16),
+            pltpu.VMEM((width, 2 * rows), BF16),
             pltpu.VMEM((rows, latent), F32),
+            pltpu.VMEM((rows, width), F32),
         ],
-        40,
     )
 
     def pair(keep, send, tied=None):
@@ -385,23 +367,8 @@
         outs = [((depth, lanes), BF16)] * held
         return call(owner_kernel, "owner", (a0, swap(a2, "grp", 2)), [VMEM] * 2, outs, tied=tied)
 
-    far = (keep, send)
-    keep, send, lat, d_rope = call(
-        functools.partial(second_kernel, scale),
-        "second",
-        (qd, cat, delta, kt, pb, o_lat, dq),
-        [VMEM] * 7,
-        [
-            ((2, depth, half), BF16),
-            ((2, depth, half), BF16),
-            ((rows, 2 * latent), BF16),
-            ((rows, rope), BF16),
-        ],
-        [pltpu.VMEM((rows, latent), BF16), pltpu.VMEM((rows, width), F32)],
-        28,
-    )
-    lat, *far = pair(*far, tied=lat)
-    near = pair(keep, send)
+    far = pair(far_keep, far_send)
+    lat, *near = pair(near_keep, near_send, tied=lat)
     far = owner(*far)
     lat = seq_swap(lat.reshape(peers, share, queries, 2 * latent))
     (res,) = call(

time: 232 us -> 228 us (0.983)
  Pallas kernels: 34.4 us -> 52.7 us
  local copies, waits for them, and re-layouts: 30.4 us -> 17.1 us
  starting transfers between devices: 62.6 us -> 49.4 us
  waiting for transfers between devices: 101 us -> 105 us
    pallas_call x12, Pallas kernels: 34.4 us -> 52.7 us  [call(): pl.pallas_call(body, out_shape=out_shape, in_specs=specs, out_specs=out_s...]
    unnamed x76 -> x74, local copies, waits for them, and re-layouts: 27.2 us -> 14.7 us
    all_to_all x4, starting transfers between devices: 27.6 us -> 18 us  [seq_swap(): return lax.all_to_all(x, 'seq', split_axis=0, concat_axis=0, tiled=True)]
    ppermute x27, starting transfers between devices: 34.9 us -> 31.4 us  [swap(): return lax.ppermute(x, axis, [(i, i ^ bit) for i in range(n)])]
    ppermute x27, waiting for transfers between devices: 92.4 us -> 95.8 us  [swap(): return lax.ppermute(x, axis, [(i, i ^ bit) for i in range(n)])]
  transfers between devices with their start and end apart: 31 -> 31, of which waited for: 13 -> 11; matrix products, arithmetic and copies ran while one was open for 1% -> 3% of each run, Pallas kernels for 7% -> 11%
where the time goes in v1:
time: 228 us; the launch traced here: 227 us
  waiting for transfers between devices  105 us (46%)
  Pallas kernels  52.7 us (23%)
  starting transfers between devices  49.4 us (22%)
  local copies, waits for them, and re-layouts  17.1 us (8%)
  other arithmetic  2.38 us (1%)
    ppermute x27, waiting for transfers between devices, swap(): return lax.ppermute(x, axis, [(i, i ^ bit) for i in range(n)])  95.8 us
    pallas_call x12, Pallas kernels, call(): pl.pallas_call(body, out_shape=out_shape, in_specs=specs, out_specs=out_s...  52.7 us
    ppermute x27, starting transfers between devices, swap(): return lax.ppermute(x, axis, [(i, i ^ bit) for i in range(n)])  31.4 us
    all_to_all x4, starting transfers between devices, seq_swap(): return lax.all_to_all(x, 'seq', split_axis=0, concat_axis=0, tiled=True)  18 us
    unnamed x74, local copies, waits for them, and re-layouts  14.7 us
    all_to_all x4, waiting for transfers between devices, seq_swap(): return lax.all_to_all(x, 'seq', split_axis=0, concat_axis=0, tiled=True)  8.96 us
  transfers between devices with their start and end apart: 31, of which 11 were waited for; matrix products, arithmetic and copies ran while one was open for 3% of the time, Pallas kernels for 11%

profile of v1, /device:TPU:0, one launch (start us, length us, event | category | flops | bytes accessed | tf_op | source)
XLA Modules:
  0.0 227.4 jit_solution(4365513146476301945)
XLA Ops:
  0.6 3.0 %collective-permute-start = (s32[1,64]{1,0:T(1,128)}, s32[1,64]{1,0:T(1,128)S(1)}, u32[]{:S(2)}, u32[]{:S(2)}) collective-permute-start(s32[1,64]{1,0:T(1,128)} %own.1), channel_id=1, source_target_pairs={{0,4},{4,0},{8,12},{12,8},{16,20},{20,16},{24,28},{28,24},{1,5},{5... | collective-permute-start | bytes 776 | tf_op jit(solution)/shard_map/ppermute | solution.py:57
  3.7 1.4 reshape.32
  6.2 1.1 pad_maximum_fusion.refs_0_
  7.8 1.2 after.1
  9.0 4.9 %all-to-all-start = ((bf16[32,160,128]{2,1,0:T(8,128)(2,1)}), bf16[32,160,128]{2,1,0:T(8,128)(2,1)S(1)}, u32[]{:S(2)}, u32[]{:S(2)}) async-start(bf16[32,160,128]{2,1,0:T(8,128)(2,1)} %get-tuple-element.28), calls=%async_computation | async-start | bytes 2621440 | tf_op jit(solution)/shard_map/all_to_all | solution.py:61
  14.5 2.0 cut.1.refs_0_
  16.5 2.9 %collective-permute-start.2 = (bf16[144,1024]{1,0:T(8,128)(2,1)}, bf16[144,1024]{1,0:T(8,128)(2,1)S(1)}, u32[]{:S(2)}, u32[]{:S(2)}) collective-permute-start(bf16[144,1024]{1,0:T(8,128)(2,1)} %cut.1.refs_0_), channel_id=1, source_target_pairs={{0,16},{4,20},{8,24},{12,28},{16,0},{20,4},{24,8},{28,12},{1,17},{... | collective-permute-start | bytes 884744 | tf_op jit(solution)/shard_map/ppermute | solution.py:57
  19.4 1.5 collective-permute-start.1
  20.9 36.7 %collective-permute-done.2.refs_2_ = bf16[144,1024]{1,0:T(8,128)(2,1)S(1)} collective-permute-done((bf16[144,1024]{1,0:T(8,128)(2,1)}, bf16[144,1024]{1,0:T(8,128)(2,1)S(1)}, u32[]{:S(2)}, u32[]{:S(2)}) %collective-permute-start.2) | collective-permute-done | bytes 294944 | tf_op jit(solution)/shard_map/ppermute | solution.py:57
  57.6 1.1 copy-done
  58.7 2.7 %expand.1 = bf16[8,4,16,1024]{3,2,1,0:T(8,128)(2,1)} custom-call(bf16[8,4,160,128]{3,2,1,0:T(8,128)(2,1)} %bitcast.30), custom_call_target="tpu_custom_call" | custom-call | tf_op jit(solution)/shard_map/expand/pallas_call | solution.py:35
  61.4 4.3 %all-to-all-start.1 = ((bf16[8,4,16,1024]{3,2,1,0:T(8,128)(2,1)}), bf16[8,4,16,1024]{3,2,1,0:T(8,128)(2,1)S(1)}, u32[]{:S(2)}, u32[]{:S(2)}) async-start(bf16[8,4,16,1024]{3,2,1,0:T(8,128)(2,1)} %expand.1), calls=%async_computation.1 | async-start | bytes 2097152 | tf_op jit(solution)/shard_map/all_to_all | solution.py:61
  66.6 4.9 %gather.1 = (bf16[144,2048]{1,0:T(8,128)(2,1)}, bf16[144,2048]{1,0:T(8,128)(2,1)}) custom-call(s32[2]{0:T(128)} %pad_add_fusion.3.ids, s32[1,64]{1,0:T(1,128)} %own.1, s32[1,64]{1,0:T(1,128)} %get-tuple-element.29.other, bf16[144,1024]{1,0:T(8,128)(2,1)} %cut.1.refs_0_, bf16[144,1024]{1,0:T(8,128)(2,1)} %copy-done.15, bf16[144,1024]{1,0:T(8,128)(2,1)} %copy-done.14, ...), custom_call_target="tpu_custom_call" | custom-call | tf_op jit(solution)/shard_map/gather/pallas_call | solution.py:35
  71.5 2.0 collective-permute-start.7
  73.5 1.5 collective-permute-start.5
  75.0 17.4 %collective-permute-done.7.refs_4_ = bf16[144,2048]{1,0:T(8,128)(2,1)S(1)} collective-permute-done((bf16[144,2048]{1,0:T(8,128)(2,1)}, bf16[144,2048]{1,0:T(8,128)(2,1)S(1)}, u32[]{:S(2)}, u32[]{:S(2)}) %collective-permute-start.7) | collective-permute-done | bytes 589856 | tf_op jit(solution)/shard_map/ppermute | solution.py:57
  92.4 1.5 collective-permute-start.9
  94.4 12.6 %collective-permute-done.9.refs_6_ = bf16[144,2048]{1,0:T(8,128)(2,1)S(1)} collective-permute-done((bf16[144,2048]{1,0:T(8,128)(2,1)S(1)}, bf16[144,2048]{1,0:T(8,128)(2,1)S(1)}, u32[]{:S(2)}, u32[]{:S(2)}) %collective-permute-start.9) | collective-permute-done | bytes 589856 | tf_op jit(solution)/shard_map/ppermute | solution.py:57
  107.5 3.2 %collective-permute-done.11 = s32[2,64]{1,0:T(2,128)S(1)} collective-permute-done((s32[2,64]{1,0:T(2,128)S(1)}, s32[2,64]{1,0:T(2,128)S(1)}, u32[]{:S(2)}, u32[]{:S(2)}) %collective-permute-start.11) | collective-permute-done | bytes 544 | tf_op jit(solution)/shard_map/ppermute | solution.py:57
  110.7 2.8 %collective-permute-start.12 = (s32[4,64]{1,0:T(4,128)S(1)}, s32[4,64]{1,0:T(4,128)S(1)}, u32[]{:S(2)}, u32[]{:S(2)}) collective-permute-start(s32[4,64]{1,0:T(4,128)S(1)} %pad_add_fusion.1), channel_id=1, source_target_pairs={{0,16},{4,20},{8,24},{12,28},{16,0},{20,4},{24,8},{28,12},{1,17},{... | collective-permute-start | bytes 3080 | tf_op jit(solution)/shard_map/ppermute | solution.py:57
  114.2 1.1 collective-permute-done.12
  115.9 0.9 copy-done.11
  117.6 0.9 copy-done.2
  118.5 23.1 %attend.1 = (bf16[2,144,2048]{2,1,0:T(8,128)(2,1)}, bf16[2,144,2048]{2,1,0:T(8,128)(2,1)}, bf16[2,144,2048]{2,1,0:T(8,128)(2,1)}, bf16[2,144,2048]{2,1,0:T(8,128...) custom-call(s32[2]{0:T(128)} %pad_add_fusion.3.ids, s32[16,32]{1,0:T(8,128)} %sel.1, ...), custom_call_target="tpu_custom_call" | custom-call | tf_op jit(solution)/shard_map/attend/pallas_call | solution.py:35
  142.1 2.5 %collective-permute-done.13.refs_2_ = bf16[2,144,2048]{2,1,0:T(8,128)(2,1)S(1)} collective-permute-done((bf16[2,144,2048]{2,1,0:T(8,128)(2,1)}, bf16[2,144,2048]{2,1,0:T(8,128)(2,1)S(1)}, u32[]{:S(2)}, u32[]{:S(2)}) %collective-permute-start.13) | collective-permute-done | bytes 1179680 | tf_op jit(solution)/shard_map/ppermute | solution.py:57
  144.7 1.1 copy-done.4
  145.7 2.8 %pair.2 = (bf16[512,1024]{1,0:T(8,128)(2,1)}, bf16[144,2048]{1,0:T(8,128)(2,1)}, bf16[144,2048]{1,0:T(8,128)(2,1)}) custom-call(bf16[512,1024]{1,0:T(8,128)(2,1)} %get-tuple-element.32.refs_0_, bf16[2,144,2048]{2,1,0:T(8,128)(2,1)} %get-tuple-element.33.refs_1_, bf16[2,144,2048]{2,1,0:T(8,128)(2,1)} %copy-done.4), custom_call_target="tpu_custom_call", output_to_operand_aliasing={{0}: (0, {})} | custom-call | tf_op jit(solution)/shard_map/pair/pallas_call | solution.py:35
  148.5 5.4 %all-to-all-start.2 = ((bf16[8,4,16,1024]{3,2,1,0:T(8,128)(2,1)}), bf16[8,4,16,1024]{3,2,1,0:T(8,128)(2,1)S(1)}, u32[]{:S(2)}, u32[]{:S(2)}) async-start(bf16[8,4,16,1024]{3,2,1,0:T(8,128)(2,1)} %bitcast.32), calls=%async_computation.2 | async-start | bytes 2097152 | tf_op jit(solution)/shard_map/all_to_all | solution.py:61
  154.0 1.0 copy-done.3
  155.0 2.8 %pair.3 = (bf16[144,2048]{1,0:T(8,128)(2,1)}, bf16[144,2048]{1,0:T(8,128)(2,1)}) custom-call(bf16[2,144,2048]{2,1,0:T(8,128)(2,1)} %get-tuple-element.44.keep, bf16[2,144,2048]{2,1,0:T(8,128)(2,1)} %copy-done.3), custom_call_target="tpu_custom_call" | custom-call | tf_op jit(solution)/shard_map/pair/pallas_call | solution.py:35
  157.8 1.5 collective-permute-start.19
  159.8 14.4 %collective-permute-done.19.got = bf16[144,2048]{1,0:T(8,128)(2,1)S(1)} collective-permute-done((bf16[144,2048]{1,0:T(8,128)(2,1)}, bf16[144,2048]{1,0:T(8,128)(2,1)S(1)}, u32[]{:S(2)}, u32[]{:S(2)}) %collective-permute-start.19) | collective-permute-done | bytes 589856 | tf_op jit(solution)/shard_map/ppermute | solution.py:57
  175.0 2.1 owner.3
  177.1 3.0 %collective-permute-start.20 = (bf16[144,512]{1,0:T(8,128)(2,1)}, bf16[144,512]{1,0:T(8,128)(2,1)S(1)}, u32[]{:S(2)}, u32[]{:S(2)}) collective-permute-start(bf16[144,512]{1,0:T(8,128)(2,1)} %get-tuple-element.48), channel_id=1, source_target_pairs={{0,16},{4,20},{8,24},{12,28},{16,0},{20,4},{24,8},{28,12},{1,17},{... | collective-permute-start | bytes 442376 | tf_op jit(solution)/shard_map/ppermute | solution.py:57
  180.1 1.5 collective-permute-start.21
  181.5 3.3 %collective-permute-start.22 = (bf16[144,512]{1,0:T(8,128)(2,1)}, bf16[144,512]{1,0:T(8,128)(2,1)S(1)}, u32[]{:S(2)}, u32[]{:S(2)}) collective-permute-start(bf16[144,512]{1,0:T(8,128)(2,1)} %get-tuple-element.50), channel_id=1, source_target_pairs={{0,24},{4,28},{8,16},{12,20},{16,8},{20,12},{24,0},{28,4},{1,25},{... | collective-permute-start | bytes 442376 | tf_op jit(solution)/shard_map/ppermute | solution.py:57
  184.8 9.0 %all-to-all-done.2.lat = bf16[8,4,16,1024]{3,2,1,0:T(8,128)(2,1)S(1)} async-done(((bf16[8,4,16,1024]{3,2,1,0:T(8,128)(2,1)}), bf16[8,4,16,1024]{3,2,1,0:T(8,128)(2,1)S(1)}, u32[]{:S(2)}, u32[]{:S(2)}) %all-to-all-start.2) | async-done | bytes 1048608 | tf_op jit(solution)/shard_map/all_to_all | solution.py:61
  193.8 1.0 copy-done.1
  194.8 2.8 %reduce.1.refs_0_ = bf16[8,4,16,256]{3,2,1,0:T(8,128)(2,1)} custom-call(bf16[8,4,160,128]{3,2,1,0:T(8,128)(2,1)} %bitcast.31, bf16[8,4,16,1024]{3,2,1,0:T(8,128)(2,1)} %copy-done.1), custom_call_target="tpu_custom_call" | custom-call | tf_op jit(solution)/shard_map/reduce/pallas_call | solution.py:35
  198.3 2.1 owner.2
  200.5 1.4 collective-permute-start.15
  201.9 2.1 collective-permute-start.17
  204.0 3.4 %all-to-all-start.3 = ((bf16[8,4,16,256]{3,2,1,0:T(8,128)(2,1)}), bf16[8,4,16,256]{3,2,1,0:T(8,128)(2,1)S(1)}, u32[]{:S(2)}, u32[]{:S(2)}) async-start(bf16[8,4,16,256]{3,2,1,0:T(8,128)(2,1)} %get-tuple-element.38), calls=%async_computation.3 | async-start | bytes 524288 | tf_op jit(solution)/shard_map/all_to_all | solution.py:61
  207.6 2.3 %collective-permute-done.17.refs_3_ = bf16[144,512]{1,0:T(8,128)(2,1)S(1)} collective-permute-done((bf16[144,512]{1,0:T(8,128)(2,1)}, bf16[144,512]{1,0:T(8,128)(2,1)S(1)}, u32[]{:S(2)}, u32[]{:S(2)}) %collective-permute-start.17) | collective-permute-done | bytes 147488 | tf_op jit(solution)/shard_map/ppermute | solution.py:57
  210.6 3.5 %scatter.1.refs_0_ = bf16[144,1024]{1,0:T(8,128)(2,1)} custom-call(s32[2]{0:T(128)} %pad_add_fusion.3.ids, s32[8,64]{1,0:T(8,128)} %pad_add_fusion.refs_8_.rows, bf16[144,512]{1,0:T(8,128)(2,1)} %get-tuple-element.40.refs_0_, bf16[144,512]{1,0:T(8,128)(2,1)} %copy-done.24, bf16[144,512]{1,0:T(8,128)(2,1)} %copy-done.25, bf16[144,512]{1,0:T(8,128)(2,1)} %copy-done.26, ...), custom_call_target="tpu_custom_call" | custom-call | tf_op jit(solution)/shard_map/scatter/pallas_call | solution.py:35
  214.0 1.5 collective-permute-start.25
  215.5 5.4 %collective-permute-done.25.refs_2_ = bf16[144,1024]{1,0:T(8,128)(2,1)S(1)} collective-permute-done((bf16[144,1024]{1,0:T(8,128)(2,1)}, bf16[144,1024]{1,0:T(8,128)(2,1)S(1)}, u32[]{:S(2)}, u32[]{:S(2)}) %collective-permute-start.25) | collective-permute-done | bytes 294944 | tf_op jit(solution)/shard_map/ppermute | solution.py:57
  224.6 2.8 %assemble.1 = f32[576,1024]{1,0:T(8,128)} custom-call(s32[2]{0:T(128)} %pad_add_fusion.3.ids, bf16[144,1024]{1,0:T(8,128)(2,1)} %scatter.1.refs_0_, bf16[144,1024]{1,0:T(8,128)(2,1)} %copy-done.18, bf16[144,1024]{1,0:T(8,128)(2,1)} %copy-done.17, bf16[144,1024]{1,0:T(8,128)(2,1)} %copy-done.19), custom_call_target="tpu_custom_call" | custom-call | tf_op jit(solution)/shard_map/assemble/pallas_call | solution.py:35
  (110 shorter events, 13.3 us)
Async XLA Ops:
  0.6 4.6 %copy-start.13 = (bf16[32,8192]{1,0:T(8,128)(2,1)S(1)}, bf16[32,8192]{1,0:T(8,128)(2,1)}, u32[]{:S(2)}) copy-start(bf16[32,8192]{1,0:T(8,128)(2,1)} %param.12) | copy-start | bytes 1572868
  0.6 6.7 %collective-permute-start = (s32[1,64]{1,0:T(1,128)}, s32[1,64]{1,0:T(1,128)S(1)}, u32[]{:S(2)}, u32[]{:S(2)}) collective-permute-start(s32[1,64]{1,0:T(1,128)} %own.1), channel_id=1, source_target_pairs={{0,4},{4,0},{8,12},{12,8},{16,20},{20,16},{24,28},{28,24},{1,5},{5... | collective-permute-start | bytes 776 | tf_op jit(solution)/shard_map/ppermute | solution.py:57
  9.0 48.6 %all-to-all-start = ((bf16[32,160,128]{2,1,0:T(8,128)(2,1)}), bf16[32,160,128]{2,1,0:T(8,128)(2,1)S(1)}, u32[]{:S(2)}, u32[]{:S(2)}) async-start(bf16[32,160,128]{2,1,0:T(8,128)(2,1)} %get-tuple-element.28), calls=%async_computation | async-start | bytes 2621440 | tf_op jit(solution)/shard_map/all_to_all | solution.py:61
  16.5 41.1 %collective-permute-start.2 = (bf16[144,1024]{1,0:T(8,128)(2,1)}, bf16[144,1024]{1,0:T(8,128)(2,1)S(1)}, u32[]{:S(2)}, u32[]{:S(2)}) collective-permute-start(bf16[144,1024]{1,0:T(8,128)(2,1)} %cut.1.refs_0_), channel_id=1, source_target_pairs={{0,16},{4,20},{8,24},{12,28},{16,0},{20,4},{24,8},{28,12},{1,17},{... | collective-permute-start | bytes 884744 | tf_op jit(solution)/shard_map/ppermute | solution.py:57
  19.4 46.3 %collective-permute-start.1 = (bf16[144,1024]{1,0:T(8,128)(2,1)}, bf16[144,1024]{1,0:T(8,128)(2,1)S(1)}, u32[]{:S(2)}, u32[]{:S(2)}) collective-permute-start(bf16[144,1024]{1,0:T(8,128)(2,1)} %cut.1.refs_0_), channel_id=1, source_target_pairs={{0,8},{4,12},{8,0},{12,4},{16,24},{20,28},{24,16},{28,20},{1,9},{5... | collective-permute-start | bytes 884744 | tf_op jit(solution)/shard_map/ppermute | solution.py:57
  57.6 8.2 %copy-start.14 = (bf16[144,1024]{1,0:T(8,128)(2,1)}, bf16[144,1024]{1,0:T(8,128)(2,1)S(1)}, u32[]{:S(2)}) copy-start(bf16[144,1024]{1,0:T(8,128)(2,1)S(1)} %collective-permute-done.2.refs_2_) | copy-start | bytes 884740
  57.6 8.2 %collective-permute-start.3 = (bf16[144,1024]{1,0:T(8,128)(2,1)S(1)}, bf16[144,1024]{1,0:T(8,128)(2,1)S(1)}, u32[]{:S(2)}, u32[]{:S(2)}) collective-permute-start(bf16[144,1024]{1,0:T(8,128)(2,1)S(1)} %collective-permute-done.2.refs_2_), channel_id=1, source_target_pairs={{0,8},{4,12},{8,0},{12,4},{16,24},{20,28},{24,16},{28,20},{1,9},{5... | collective-permute-start | bytes 884744 | tf_op jit(solution)/shard_map/ppermute | solution.py:57
  61.4 45.6 %copy-start.31 = (s32[1,64]{1,0:T(1,128)S(1)}, s32[1,64]{1,0:T(1,128)}, u32[]{:S(2)}) copy-start(s32[1,64]{1,0:T(1,128)} %own.1) | copy-start | bytes 772
  61.4 45.6 %copy-start.32 = (s32[1,64]{1,0:T(1,128)S(1)}, s32[1,64]{1,0:T(1,128)}, u32[]{:S(2)}) copy-start(s32[1,64]{1,0:T(1,128)} %get-tuple-element.29.other) | copy-start | bytes 772
  61.4 52.1 %copy-start.27 = (bf16[16,32,64]{2,1,0:T(8,128)(2,1)S(1)}, bf16[16,32,64]{2,1,0:T(8,128)(2,1)}, u32[]{:S(2)}) copy-start(bf16[16,32,64]{2,1,0:T(8,128)(2,1)} %param.9) | copy-start | bytes 196612
  61.4 56.1 %all-to-all-start.1 = ((bf16[8,4,16,1024]{3,2,1,0:T(8,128)(2,1)}), bf16[8,4,16,1024]{3,2,1,0:T(8,128)(2,1)S(1)}, u32[]{:S(2)}, u32[]{:S(2)}) async-start(bf16[8,4,16,1024]{3,2,1,0:T(8,128)(2,1)} %expand.1), calls=%async_computation.1 | async-start | bytes 2097152 | tf_op jit(solution)/shard_map/all_to_all | solution.py:61
  71.5 20.9 %collective-permute-start.7 = (bf16[144,2048]{1,0:T(8,128)(2,1)}, bf16[144,2048]{1,0:T(8,128)(2,1)S(1)}, u32[]{:S(2)}, u32[]{:S(2)}) collective-permute-start(bf16[144,2048]{1,0:T(8,128)(2,1)} %get-tuple-element.31), channel_id=1, source_target_pairs={{0,4},{4,0},{8,12},{12,8},{16,20},{20,16},{24,28},{28,24},{1,5},{5... | collective-permute-start | bytes 1769480 | tf_op jit(solution)/shard_map/ppermute | solution.py:57
  73.5 20.9 %collective-permute-start.5 = (bf16[144,2048]{1,0:T(8,128)(2,1)}, bf16[144,2048]{1,0:T(8,128)(2,1)S(1)}, u32[]{:S(2)}, u32[]{:S(2)}) collective-permute-start(bf16[144,2048]{1,0:T(8,128)(2,1)} %get-tuple-element.30.refs_0_), channel_id=1, source_target_pairs={{0,2},{1,3},{2,0},{3,1},{4,6},{5,7},{6,4},{7,5},{8,10},{9,11},{10,... | collective-permute-start | bytes 1769480 | tf_op jit(solution)/shard_map/ppermute | solution.py:57
  92.4 25.2 %copy-start.7 = (bf16[144,2048]{1,0:T(8,128)(2,1)}, bf16[144,2048]{1,0:T(8,128)(2,1)S(1)}, u32[]{:S(2)}) copy-start(bf16[144,2048]{1,0:T(8,128)(2,1)S(1)} %collective-permute-done.7.refs_4_) | copy-start | bytes 1769476
  92.4 14.7 %collective-permute-start.9 = (bf16[144,2048]{1,0:T(8,128)(2,1)S(1)}, bf16[144,2048]{1,0:T(8,128)(2,1)S(1)}, u32[]{:S(2)}, u32[]{:S(2)}) collective-permute-start(bf16[144,2048]{1,0:T(8,128)(2,1)S(1)} %collective-permute-done.7.refs_4_), channel_id=1, source_target_pairs={{0,2},{1,3},{2,0},{3,1},{4,6},{5,7},{6,4},{7,5},{8,10},{9,11},{10,... | collective-permute-start | bytes 1769480 | tf_op jit(solution)/shard_map/ppermute | solution.py:57
  93.9 22.0 %collective-permute-start.4 = (bf16[144,2048]{1,0:T(8,128)(2,1)}, bf16[144,2048]{1,0:T(8,128)(2,1)S(1)}, u32[]{:S(2)}, u32[]{:S(2)}) collective-permute-start(bf16[144,2048]{1,0:T(8,128)(2,1)} %get-tuple-element.30.refs_0_), channel_id=1, source_target_pairs={{0,1},{1,0},{2,3},{3,2},{4,5},{5,4},{6,7},{7,6},{8,9},{9,8},{10,11... | collective-permute-start | bytes 1769480 | tf_op jit(solution)/shard_map/ppermute | solution.py:57
  93.9 22.0 %collective-permute-start.8 = (bf16[144,2048]{1,0:T(8,128)(2,1)S(1)}, bf16[144,2048]{1,0:T(8,128)(2,1)S(1)}, u32[]{:S(2)}, u32[]{:S(2)}) collective-permute-start(bf16[144,2048]{1,0:T(8,128)(2,1)S(1)} %collective-permute-done.7.refs_4_), channel_id=1, source_target_pairs={{0,1},{1,0},{2,3},{3,2},{4,5},{5,4},{6,7},{7,6},{8,9},{9,8},{10,11... | collective-permute-start | bytes 1769480 | tf_op jit(solution)/shard_map/ppermute | solution.py:57
  94.4 23.2 %copy-start.8 = (bf16[144,2048]{1,0:T(8,128)(2,1)}, bf16[144,2048]{1,0:T(8,128)(2,1)S(1)}, u32[]{:S(2)}) copy-start(bf16[144,2048]{1,0:T(8,128)(2,1)S(1)} %collective-permute-done.5.refs_2_) | copy-start | bytes 1769476
  94.4 21.5 %collective-permute-start.6 = (bf16[144,2048]{1,0:T(8,128)(2,1)S(1)}, bf16[144,2048]{1,0:T(8,128)(2,1)S(1)}, u32[]{:S(2)}, u32[]{:S(2)}) collective-permute-start(bf16[144,2048]{1,0:T(8,128)(2,1)S(1)} %collective-permute-done.5.refs_2_), channel_id=1, source_target_pairs={{0,1},{1,0},{2,3},{3,2},{4,5},{5,4},{6,7},{7,6},{8,9},{9,8},{10,11... | collective-permute-start | bytes 1769480 | tf_op jit(solution)/shard_map/ppermute | solution.py:57
  107.0 10.6 %copy-start.9 = (bf16[144,2048]{1,0:T(8,128)(2,1)}, bf16[144,2048]{1,0:T(8,128)(2,1)S(1)}, u32[]{:S(2)}) copy-start(bf16[144,2048]{1,0:T(8,128)(2,1)S(1)} %collective-permute-done.9.refs_6_) | copy-start | bytes 1769476
  107.0 10.5 %collective-permute-start.10 = (bf16[144,2048]{1,0:T(8,128)(2,1)S(1)}, bf16[144,2048]{1,0:T(8,128)(2,1)}, u32[]{:S(2)}, u32[]{:S(2)}) collective-permute-start(bf16[144,2048]{1,0:T(8,128)(2,1)S(1)} %collective-permute-done.9.refs_6_), channel_id=1, source_target_pairs={{0,1},{1,0},{2,3},{3,2},{4,5},{5,4},{6,7},{7,6},{8,9},{9,8},{10,11... | collective-permute-start | bytes 1769480 | tf_op jit(solution)/shard_map/ppermute | solution.py:57
  107.1 3.6 %collective-permute-start.11 = (s32[2,64]{1,0:T(2,128)S(1)}, s32[2,64]{1,0:T(2,128)S(1)}, u32[]{:S(2)}, u32[]{:S(2)}) collective-permute-start(s32[2,64]{1,0:T(2,128)S(1)} %pad_add_fusion.2), channel_id=1, source_target_pairs={{0,8},{4,12},{8,0},{12,4},{16,24},{20,28},{24,16},{28,20},{1,9},{5... | collective-permute-start | bytes 1544 | tf_op jit(solution)/shard_map/ppermute | solution.py:57
  110.7 4.5 %collective-permute-start.12 = (s32[4,64]{1,0:T(4,128)S(1)}, s32[4,64]{1,0:T(4,128)S(1)}, u32[]{:S(2)}, u32[]{:S(2)}) collective-permute-start(s32[4,64]{1,0:T(4,128)S(1)} %pad_add_fusion.1), channel_id=1, source_target_pairs={{0,16},{4,20},{8,24},{12,28},{16,0},{20,4},{24,8},{28,12},{1,17},{... | collective-permute-start | bytes 3080 | tf_op jit(solution)/shard_map/ppermute | solution.py:57
  141.6 3.1 %collective-permute-start.13 = (bf16[2,144,2048]{2,1,0:T(8,128)(2,1)}, bf16[2,144,2048]{2,1,0:T(8,128)(2,1)S(1)}, u32[]{:S(2)}, u32[]{:S(2)}) collective-permute-start(bf16[2,144,2048]{2,1,0:T(8,128)(2,1)} %get-tuple-element.34), channel_id=1, source_target_pairs={{0,1},{1,0},{2,3},{3,2},{4,5},{5,4},{6,7},{7,6},{8,9},{9,8},{10,11... | collective-permute-start | bytes 3538952 | tf_op jit(solution)/shard_map/ppermute | solution.py:57
  141.6 12.3 %collective-permute-start.18 = (bf16[2,144,2048]{2,1,0:T(8,128)(2,1)}, bf16[2,144,2048]{2,1,0:T(8,128)(2,1)S(1)}, u32[]{:S(2)}, u32[]{:S(2)}) collective-permute-start(bf16[2,144,2048]{2,1,0:T(8,128)(2,1)} %get-tuple-element.45), channel_id=1, source_target_pairs={{0,1},{1,0},{2,3},{3,2},{4,5},{5,4},{6,7},{7,6},{8,9},{9,8},{10,11... | collective-permute-start | bytes 3538952 | tf_op jit(solution)/shard_map/ppermute | solution.py:57
  148.5 45.3 %all-to-all-start.2 = ((bf16[8,4,16,1024]{3,2,1,0:T(8,128)(2,1)}), bf16[8,4,16,1024]{3,2,1,0:T(8,128)(2,1)S(1)}, u32[]{:S(2)}, u32[]{:S(2)}) async-start(bf16[8,4,16,1024]{3,2,1,0:T(8,128)(2,1)} %bitcast.32), calls=%async_computation.2 | async-start | bytes 2097152 | tf_op jit(solution)/shard_map/all_to_all | solution.py:61
  153.9 5.3 %copy-start.34 = (bf16[144,2048]{1,0:T(8,128)(2,1)S(1)}, bf16[144,2048]{1,0:T(8,128)(2,1)}, u32[]{:S(2)}) copy-start(bf16[144,2048]{1,0:T(8,128)(2,1)} %get-tuple-element.37) | copy-start | bytes 1769476
  157.8 16.4 %collective-permute-start.19 = (bf16[144,2048]{1,0:T(8,128)(2,1)}, bf16[144,2048]{1,0:T(8,128)(2,1)S(1)}, u32[]{:S(2)}, u32[]{:S(2)}) collective-permute-start(bf16[144,2048]{1,0:T(8,128)(2,1)} %get-tuple-element.47), channel_id=1, source_target_pairs={{0,2},{1,3},{2,0},{3,1},{4,6},{5,7},{6,4},{7,5},{8,10},{9,11},{10,... | collective-permute-start | bytes 1769480 | tf_op jit(solution)/shard_map/ppermute | solution.py:57
  159.3 38.3 %collective-permute-start.14 = (bf16[144,2048]{1,0:T(8,128)(2,1)S(1)}, bf16[144,2048]{1,0:T(8,128)(2,1)S(1)}, u32[]{:S(2)}, u32[]{:S(2)}) collective-permute-start(bf16[144,2048]{1,0:T(8,128)(2,1)S(1)} %copy-done.34), channel_id=1, source_target_pairs={{0,2},{1,3},{2,0},{3,1},{4,6},{5,7},{6,4},{7,5},{8,10},{9,11},{10,... | collective-permute-start | bytes 1769480 | tf_op jit(solution)/shard_map/ppermute | solution.py:57
  177.1 24.7 %collective-permute-start.20 = (bf16[144,512]{1,0:T(8,128)(2,1)}, bf16[144,512]{1,0:T(8,128)(2,1)S(1)}, u32[]{:S(2)}, u32[]{:S(2)}) collective-permute-start(bf16[144,512]{1,0:T(8,128)(2,1)} %get-tuple-element.48), channel_id=1, source_target_pairs={{0,16},{4,20},{8,24},{12,28},{16,0},{20,4},{24,8},{28,12},{1,17},{... | collective-permute-start | bytes 442376 | tf_op jit(solution)/shard_map/ppermute | solution.py:57
  180.1 21.8 %collective-permute-start.21 = (bf16[144,512]{1,0:T(8,128)(2,1)}, bf16[144,512]{1,0:T(8,128)(2,1)S(1)}, u32[]{:S(2)}, u32[]{:S(2)}) collective-permute-start(bf16[144,512]{1,0:T(8,128)(2,1)} %get-tuple-element.49), channel_id=1, source_target_pairs={{0,20},{4,16},{8,28},{12,24},{16,4},{20,0},{24,12},{28,8},{1,21},{... | collective-permute-start | bytes 442376 | tf_op jit(solution)/shard_map/ppermute | solution.py:57
  181.5 25.9 %collective-permute-start.22 = (bf16[144,512]{1,0:T(8,128)(2,1)}, bf16[144,512]{1,0:T(8,128)(2,1)S(1)}, u32[]{:S(2)}, u32[]{:S(2)}) collective-permute-start(bf16[144,512]{1,0:T(8,128)(2,1)} %get-tuple-element.50), channel_id=1, source_target_pairs={{0,24},{4,28},{8,16},{12,20},{16,8},{20,12},{24,0},{28,4},{1,25},{... | collective-permute-start | bytes 442376 | tf_op jit(solution)/shard_map/ppermute | solution.py:57
  184.8 22.6 %collective-permute-start.23 = (bf16[144,512]{1,0:T(8,128)(2,1)}, bf16[144,512]{1,0:T(8,128)(2,1)S(1)}, u32[]{:S(2)}, u32[]{:S(2)}) collective-permute-start(bf16[144,512]{1,0:T(8,128)(2,1)} %get-tuple-element.51), channel_id=1, source_target_pairs={{0,28},{4,24},{8,20},{12,16},{16,12},{20,8},{24,4},{28,0},{1,29},{... | collective-permute-start | bytes 442376 | tf_op jit(solution)/shard_map/ppermute | solution.py:57
  200.5 20.5 %copy-start.28 = (bf16[512,64]{1,0:T(8,128)(2,1)S(1)}, bf16[512,64]{1,0:T(8,128)(2,1)}, u32[]{:S(2)}) copy-start(bf16[512,64]{1,0:T(8,128)(2,1)} %get-tuple-element.39) | copy-start | bytes 196612
  200.5 7.0 %collective-permute-start.15 = (bf16[144,512]{1,0:T(8,128)(2,1)}, bf16[144,512]{1,0:T(8,128)(2,1)S(1)}, u32[]{:S(2)}, u32[]{:S(2)}) collective-permute-start(bf16[144,512]{1,0:T(8,128)(2,1)} %get-tuple-element.41), channel_id=1, source_target_pairs={{0,4},{4,0},{8,12},{12,8},{16,20},{20,16},{24,28},{28,24},{1,5},{5... | collective-permute-start | bytes 442376 | tf_op jit(solution)/shard_map/ppermute | solution.py:57
  201.8 8.1 %copy-start.20 = (bf16[144,512]{1,0:T(8,128)(2,1)}, bf16[144,512]{1,0:T(8,128)(2,1)S(1)}, u32[]{:S(2)}) copy-start(bf16[144,512]{1,0:T(8,128)(2,1)S(1)} %collective-permute-done.20.refs_4_) | copy-start | bytes 442372
  201.8 5.8 %collective-permute-start.16 = (bf16[144,512]{1,0:T(8,128)(2,1)}, bf16[144,512]{1,0:T(8,128)(2,1)S(1)}, u32[]{:S(2)}, u32[]{:S(2)}) collective-permute-start(bf16[144,512]{1,0:T(8,128)(2,1)} %get-tuple-element.42), channel_id=1, source_target_pairs={{0,8},{4,12},{8,0},{12,4},{16,24},{20,28},{24,16},{28,20},{1,9},{5... | collective-permute-start | bytes 442376 | tf_op jit(solution)/shard_map/ppermute | solution.py:57
  201.9 8.1 %copy-start.21 = (bf16[144,512]{1,0:T(8,128)(2,1)}, bf16[144,512]{1,0:T(8,128)(2,1)S(1)}, u32[]{:S(2)}) copy-start(bf16[144,512]{1,0:T(8,128)(2,1)S(1)} %collective-permute-done.21.refs_5_) | copy-start | bytes 442372
  201.9 8.1 %collective-permute-start.17 = (bf16[144,512]{1,0:T(8,128)(2,1)}, bf16[144,512]{1,0:T(8,128)(2,1)S(1)}, u32[]{:S(2)}, u32[]{:S(2)}) collective-permute-start(bf16[144,512]{1,0:T(8,128)(2,1)} %get-tuple-element.43), channel_id=1, source_target_pairs={{0,12},{4,8},{8,4},{12,0},{16,28},{20,24},{24,20},{28,16},{1,13},{... | collective-permute-start | bytes 442376 | tf_op jit(solution)/shard_map/ppermute | solution.py:57
  204.0 17.8 %all-to-all-start.3 = ((bf16[8,4,16,256]{3,2,1,0:T(8,128)(2,1)}), bf16[8,4,16,256]{3,2,1,0:T(8,128)(2,1)S(1)}, u32[]{:S(2)}, u32[]{:S(2)}) async-start(bf16[8,4,16,256]{3,2,1,0:T(8,128)(2,1)} %get-tuple-element.38), calls=%async_computation.3 | async-start | bytes 524288 | tf_op jit(solution)/shard_map/all_to_all | solution.py:61
  207.4 2.5 %copy-start.22 = (bf16[144,512]{1,0:T(8,128)(2,1)}, bf16[144,512]{1,0:T(8,128)(2,1)S(1)}, u32[]{:S(2)}) copy-start(bf16[144,512]{1,0:T(8,128)(2,1)S(1)} %collective-permute-done.22.refs_6_) | copy-start | bytes 442372
  207.4 2.5 %copy-start.23 = (bf16[144,512]{1,0:T(8,128)(2,1)}, bf16[144,512]{1,0:T(8,128)(2,1)S(1)}, u32[]{:S(2)}) copy-start(bf16[144,512]{1,0:T(8,128)(2,1)S(1)} %collective-permute-done.23.refs_7_) | copy-start | bytes 442372
  207.4 2.5 %copy-start.24 = (bf16[144,512]{1,0:T(8,128)(2,1)}, bf16[144,512]{1,0:T(8,128)(2,1)S(1)}, u32[]{:S(2)}) copy-start(bf16[144,512]{1,0:T(8,128)(2,1)S(1)} %collective-permute-done.15.refs_1_) | copy-start | bytes 442372
  207.6 2.3 %copy-start.25 = (bf16[144,512]{1,0:T(8,128)(2,1)}, bf16[144,512]{1,0:T(8,128)(2,1)S(1)}, u32[]{:S(2)}) copy-start(bf16[144,512]{1,0:T(8,128)(2,1)S(1)} %collective-permute-done.16.refs_2_) | copy-start | bytes 442372
  214.0 6.9 %collective-permute-start.25 = (bf16[144,1024]{1,0:T(8,128)(2,1)}, bf16[144,1024]{1,0:T(8,128)(2,1)S(1)}, u32[]{:S(2)}, u32[]{:S(2)}) collective-permute-start(bf16[144,1024]{1,0:T(8,128)(2,1)} %scatter.1.refs_0_), channel_id=1, source_target_pairs={{0,2},{1,3},{2,0},{3,1},{4,6},{5,7},{6,4},{7,5},{8,10},{9,11},{10,... | collective-permute-start | bytes 884744 | tf_op jit(solution)/shard_map/ppermute | solution.py:57
  215.5 7.6 %collective-permute-start.24 = (bf16[144,1024]{1,0:T(8,128)(2,1)}, bf16[144,1024]{1,0:T(8,128)(2,1)S(1)}, u32[]{:S(2)}, u32[]{:S(2)}) collective-permute-start(bf16[144,1024]{1,0:T(8,128)(2,1)} %scatter.1.refs_0_), channel_id=1, source_target_pairs={{0,1},{1,0},{2,3},{3,2},{4,5},{5,4},{6,7},{7,6},{8,9},{9,8},{10,11... | collective-permute-start | bytes 884744 | tf_op jit(solution)/shard_map/ppermute | solution.py:57
  221.0 2.2 copy-start.17
  221.0 2.2 collective-permute-start.26
  (18 other events, 16.2 us)

commit v2 on v1

--- a/solution.py
+++ b/solution.py
@@ -18,7 +18,7 @@
 BF16 = jnp.bfloat16
 
 
-def call(kernel, name, args, specs, outs, scratch=(), tied=None):
+def call(kernel, name, args, specs, outs, scratch=(), mib=16, tied=None):
     out_shape = [jax.ShapeDtypeStruct(s, d) for s, d in outs]
     out_specs = [VMEM] * len(outs)
     aliases = {}
@@ -39,7 +39,7 @@
         out_specs=out_specs,
         scratch_shapes=list(scratch),
         input_output_aliases=aliases,
-        compiler_params=pltpu.CompilerParams(vmem_limit_bytes=60 * 2**20),
+        compiler_params=pltpu.CompilerParams(vmem_limit_bytes=mib * 2**20),
         name=name,
     )(*args)
 
@@ -65,8 +65,8 @@
     return [pieces[0]] + [swap(p, "seq", k) for k, p in enumerate(pieces) if k > 0]
 
 
-def copy_kernel(x, out):
-    out[...] = x[...]
+def tie_kernel(*refs):
+    pass
 
 
 def cut_kernel(ids, cache, out):
@@ -293,6 +293,11 @@
 
     row1 = swap(slot_blocks, "seq", 1)
     (c0,) = call(cut_kernel, "cut", (ids, cache.T), [SMEM, VMEM], [((depth, tokens), BF16)])
+    c2 = swap(c0, "seq", 4)
+    c1 = swap(c0, "seq", 2)
+    asked = jnp.concatenate([slot_blocks, row1], axis=0)
+    for bit in (2, 4):
+        asked = jnp.concatenate([asked, swap(asked, "seq", bit)], axis=0)
 
     n_rows = w_uk.shape[1] // latent
     l_rows = w_uv.shape[1] // value
@@ -307,9 +312,7 @@
         ],
         axis=1,
     )
-    pack, row1 = call(
-        copy_kernel, "after", (row1,), [VMEM], [(row1.shape, jnp.int32)], tied=pack
-    )
+    (pack,) = call(tie_kernel, "after", (c2, asked), [ANY] * 2, [], tied=pack)
     pack = seq_swap(pack).reshape(peers, share, -1, LANES)
     sizes = (n_rows * tiles, l_rows, queries, tiles, latent)
     (lat,) = call(
@@ -321,8 +324,6 @@
     )
     qd = seq_swap(lat).reshape(rows, 2 * latent)
 
-    c2 = swap(c0, "seq", 4)
-    c1 = swap(c0, "seq", 2)
     c3 = swap(c2, "seq", 2)
     away, k0 = call(
         functools.partial(gather_kernel, per_peer),
@@ -335,10 +336,6 @@
     for k in (k0, swap(away, "seq", 1)):
         k2 = swap(k, "grp", 2)
         keys += [k, swap(k, "grp", 1), k2, swap(k2, "grp", 1)]
-    asked = jnp.concatenate([slot_blocks, row1], axis=0)
-    for bit in (2, 4):
-        asked = jnp.concatenate([asked, swap(asked, "seq", bit)], axis=0)
-
     rope_rows = q_rope.transpose(1, 0, 2)
     near_keep, near_send, far_keep, far_send, lat, d_rope = call(
         functools.partial(attend_kernel, scale, per_peer),
@@ -357,19 +354,21 @@
             pltpu.VMEM((rows, latent), F32),
             pltpu.VMEM((rows, width), F32),
         ],
+        60,
     )
 
     def pair(keep, send, tied=None):
         outs = [((depth, half), BF16)] * 2
         return call(pair_kernel, "pair", (keep, swap(send, "grp", 1)), [VMEM] * 2, outs, tied=tied)
 
+
     def owner(a0, a2, tied=None):
         outs = [((depth, lanes), BF16)] * held
         return call(owner_kernel, "owner", (a0, swap(a2, "grp", 2)), [VMEM] * 2, outs, tied=tied)
 
     far = pair(far_keep, far_send)
-    lat, *near = pair(near_keep, near_send, tied=lat)
-    far = owner(*far)
+    first, *near = pair(near_keep, near_send, tied=far[0])
+    far = owner(first, far[1])
     lat = seq_swap(lat.reshape(peers, share, queries, 2 * latent))
     (res,) = call(
         functools.partial(reduce_kernel, sizes),

time: 228 us -> 204 us (0.89)
  Pallas kernels: 52.7 us -> 37.7 us
  local copies, waits for them, and re-layouts: 17.1 us -> 7.37 us
    all_to_all x4, waiting for transfers between devices: 8.96 us -> 42.9 us  [seq_swap(): return lax.all_to_all(x, 'seq', split_axis=0, concat_axis=0, tiled=True)]
    ppermute x27, waiting for transfers between devices: 95.8 us -> 63 us  [swap(): return lax.ppermute(x, axis, [(i, i ^ bit) for i in range(n)])]
    pallas_call x12, Pallas kernels: 52.7 us -> 37.7 us  [call(): pl.pallas_call(body, out_shape=out_shape, in_specs=specs, out_specs=out_s...]
    unnamed x74 -> x46, local copies, waits for them, and re-layouts: 14.7 us -> 6.07 us
  transfers between devices with their start and end apart: 31 -> 31, of which waited for: 11 -> 11; matrix products, arithmetic and copies ran while one was open for 3% -> 2% of each run, Pallas kernels for 11% -> 6%
where the time goes in v2:
time: 204 us; the launch traced here: 203 us
  waiting for transfers between devices  106 us (52%)
  starting transfers between devices  49.4 us (24%)
  Pallas kernels  37.7 us (18%)
  local copies, waits for them, and re-layouts  7.37 us (4%)
    ppermute x27, waiting for transfers between devices, swap(): return lax.ppermute(x, axis, [(i, i ^ bit) for i in range(n)])  63 us
    all_to_all x4, waiting for transfers between devices, seq_swap(): return lax.all_to_all(x, 'seq', split_axis=0, concat_axis=0, tiled=True)  42.9 us
    pallas_call x12, Pallas kernels, call(): pl.pallas_call(body, out_shape=out_shape, in_specs=specs, out_specs=out_s...  37.7 us
    ppermute x27, starting transfers between devices, swap(): return lax.ppermute(x, axis, [(i, i ^ bit) for i in range(n)])  31.4 us
    all_to_all x4, starting transfers between devices, seq_swap(): return lax.all_to_all(x, 'seq', split_axis=0, concat_axis=0, tiled=True)  17.9 us
    unnamed x46, local copies, waits for them, and re-layouts  6.07 us
  transfers between devices with their start and end apart: 31, of which 11 were waited for; matrix products, arithmetic and copies ran while one was open for 2% of the time, Pallas kernels for 6%

profile of v2, /device:TPU:0, one launch (start us, length us, event | category | flops | bytes accessed | tf_op | source)
XLA Modules:
  0.0 202.5 jit_solution(9094308127532443593)
XLA Ops:
  0.6 3.0 %collective-permute-start.1 = (s32[1,64]{1,0:T(1,128)}, s32[1,64]{1,0:T(1,128)S(1)}, u32[]{:S(2)}, u32[]{:S(2)}) collective-permute-start(s32[1,64]{1,0:T(1,128)} %own.1), channel_id=1, source_target_pairs={{0,4},{4,0},{8,12},{12,8},{16,20},{20,16},{24,28},{28,24},{1,5},{5... | collective-permute-start | bytes 776 | tf_op jit(solution)/shard_map/ppermute | solution.py:57
  3.8 1.3 copy-done.1
  5.0 0.6 cut.1.refs_0_
  5.6 2.7 %collective-permute-start = (bf16[144,1024]{1,0:T(8,128)(2,1)S(1)}, bf16[144,1024]{1,0:T(8,128)(2,1)S(1)}, u32[]{:S(2)}, u32[]{:S(2)}) collective-permute-start(bf16[144,1024]{1,0:T(8,128)(2,1)S(1)} %cut.1.refs_0_), channel_id=1, source_target_pairs={{0,16},{4,20},{8,24},{12,28},{16,0},{20,4},{24,8},{28,12},{1,17},{... | collective-permute-start | bytes 884744 | tf_op jit(solution)/shard_map/ppermute | solution.py:57
  8.3 1.6 collective-permute-start.2
  10.7 3.7 %collective-permute-done.2 = s32[2,64]{1,0:T(2,128)S(1)} collective-permute-done((s32[2,64]{1,0:T(2,128)S(1)}, s32[2,64]{1,0:T(2,128)S(1)}, u32[]{:S(2)}, u32[]{:S(2)}) %collective-permute-start.2) | collective-permute-done | bytes 544 | tf_op jit(solution)/shard_map/ppermute | solution.py:57
  14.3 2.4 %collective-permute-start.3 = (s32[4,64]{1,0:T(4,128)S(1)}, s32[4,64]{1,0:T(4,128)S(1)}, u32[]{:S(2)}, u32[]{:S(2)}) collective-permute-start(s32[4,64]{1,0:T(4,128)S(1)} %pad_add_fusion.1), channel_id=1, source_target_pairs={{0,16},{4,20},{8,24},{12,28},{16,0},{20,4},{24,8},{28,12},{1,17},{... | collective-permute-start | bytes 3080 | tf_op jit(solution)/shard_map/ppermute | solution.py:57
  16.7 1.1 pad_maximum_fusion.refs_0_
  17.9 3.6 %collective-permute-done.3 = s32[4,64]{1,0:T(4,128)S(1)} collective-permute-done((s32[4,64]{1,0:T(4,128)S(1)}, s32[4,64]{1,0:T(4,128)S(1)}, u32[]{:S(2)}, u32[]{:S(2)}) %collective-permute-start.3) | collective-permute-done | bytes 1056 | tf_op jit(solution)/shard_map/ppermute | solution.py:57
  21.5 0.6 copy-done.4
  22.1 4.8 %all-to-all-start = ((bf16[32,160,128]{2,1,0:T(8,128)(2,1)}), bf16[32,160,128]{2,1,0:T(8,128)(2,1)S(1)}, u32[]{:S(2)}, u32[]{:S(2)}) async-start(bf16[32,160,128]{2,1,0:T(8,128)(2,1)} %after.1), calls=%async_computation | async-start | bytes 2621440 | tf_op jit(solution)/shard_map/all_to_all | solution.py:61
  26.8 2.0 collective-permute-start.4
  28.9 29.6 %all-to-all-done = bf16[32,160,128]{2,1,0:T(8,128)(2,1)S(1)} async-done(((bf16[32,160,128]{2,1,0:T(8,128)(2,1)}), bf16[32,160,128]{2,1,0:T(8,128)(2,1)S(1)}, u32[]{:S(2)}, u32[]{:S(2)}) %all-to-all-start) | async-done | bytes 1310752 | tf_op jit(solution)/shard_map/all_to_all | solution.py:61
  58.5 1.4 expand.1
  59.9 4.4 %all-to-all-start.1 = ((bf16[8,4,16,1024]{3,2,1,0:T(8,128)(2,1)}), bf16[8,4,16,1024]{3,2,1,0:T(8,128)(2,1)}, u32[]{:S(2)}, u32[]{:S(2)}) async-start(bf16[8,4,16,1024]{3,2,1,0:T(8,128)(2,1)} %expand.1), calls=%async_computation.1 | async-start | bytes 2097152 | tf_op jit(solution)/shard_map/all_to_all | solution.py:61
  64.3 3.3 %gather.1 = (bf16[144,2048]{1,0:T(8,128)(2,1)S(1)}, bf16[144,2048]{1,0:T(8,128)(2,1)S(1)}) custom-call(s32[2]{0:T(128)S(1)} %pad_add_fusion.3.ids, s32[1,64]{1,0:T(1,128)S(1)} %copy-done.8, s32[1,64]{1,0:T(1,128)S(1)} %collective-permute-done.1.other, bf16[144,1024]{1,0:T(8,128)(2,1)S(1)} %cut.1.refs_0_, ...), custom_call_target="tpu_custom_call" | custom-call | tf_op jit(solution)/shard_map/gather/pallas_call | solution.py:35
  67.6 1.9 collective-permute-start.9
  69.6 1.5 collective-permute-start.7
  71.1 19.3 %collective-permute-done.9.refs_4_ = bf16[144,2048]{1,0:T(8,128)(2,1)S(1)} collective-permute-done((bf16[144,2048]{1,0:T(8,128)(2,1)S(1)}, bf16[144,2048]{1,0:T(8,128)(2,1)S(1)}, u32[]{:S(2)}, u32[]{:S(2)}) %collective-permute-start.9) | collective-permute-done | bytes 589856 | tf_op jit(solution)/shard_map/ppermute | solution.py:57
  90.4 1.5 collective-permute-start.11
  92.5 12.5 %collective-permute-done.11.refs_6_ = bf16[144,2048]{1,0:T(8,128)(2,1)S(1)} collective-permute-done((bf16[144,2048]{1,0:T(8,128)(2,1)S(1)}, bf16[144,2048]{1,0:T(8,128)(2,1)S(1)}, u32[]{:S(2)}, u32[]{:S(2)}) %collective-permute-start.11) | collective-permute-done | bytes 589856 | tf_op jit(solution)/shard_map/ppermute | solution.py:57
  104.9 0.8 copy.34
  105.8 0.7 copy-done.12
  106.8 0.9 copy-done.14
  107.7 23.1 %attend.1 = (bf16[2,144,2048]{2,1,0:T(8,128)(2,1)}, bf16[2,144,2048]{2,1,0:T(8,128)(2,1)}, bf16[2,144,2048]{2,1,0:T(8,128)(2,1)}, bf16[2,144,2048]{2,1,0:T(8,128...) custom-call(s32[2]{0:T(128)} %copy-done.6, s32[16,32]{1,0:T(8,128)} %sel.1, bf16[32,16,64]{2,1,0:T(8,128)(2,1)} %bitcast.38, ...), custom_call_target="tpu_custom_call" | custom-call | tf_op jit(solution)/shard_map/attend/pallas_call | solution.py:35
  131.3 4.6 %all-to-all-start.2 = ((bf16[8,4,16,1024]{3,2,1,0:T(8,128)(2,1)}), bf16[8,4,16,1024]{3,2,1,0:T(8,128)(2,1)S(1)}, u32[]{:S(2)}, u32[]{:S(2)}) async-start(bf16[8,4,16,1024]{3,2,1,0:T(8,128)(2,1)} %bitcast.36), calls=%async_computation.2 | async-start | bytes 2097152 | tf_op jit(solution)/shard_map/all_to_all | solution.py:61
  136.0 1.6 pair.2
  137.6 1.6 collective-permute-start.19
  139.1 1.0 pair.3
  140.1 1.3 collective-permute-start.15
  141.5 12.3 %collective-permute-done.19.got = bf16[144,2048]{1,0:T(8,128)(2,1)S(1)} collective-permute-done((bf16[144,2048]{1,0:T(8,128)(2,1)S(1)}, bf16[144,2048]{1,0:T(8,128)(2,1)S(1)}, u32[]{:S(2)}, u32[]{:S(2)}) %collective-permute-start.19) | collective-permute-done | bytes 589856 | tf_op jit(solution)/shard_map/ppermute | solution.py:57
  153.8 0.9 owner.3
  154.7 2.9 %collective-permute-start.20 = (bf16[144,512]{1,0:T(8,128)(2,1)}, bf16[144,512]{1,0:T(8,128)(2,1)}, u32[]{:S(2)}, u32[]{:S(2)}) collective-permute-start(bf16[144,512]{1,0:T(8,128)(2,1)} %get-tuple-element.44), channel_id=1, source_target_pairs={{0,16},{4,20},{8,24},{12,28},{16,0},{20,4},{24,8},{28,12},{1,17},{... | collective-permute-start | bytes 442376 | tf_op jit(solution)/shard_map/ppermute | solution.py:57
  157.5 1.5 collective-permute-start.21
  159.0 3.3 %collective-permute-start.22 = (bf16[144,512]{1,0:T(8,128)(2,1)}, bf16[144,512]{1,0:T(8,128)(2,1)}, u32[]{:S(2)}, u32[]{:S(2)}) collective-permute-start(bf16[144,512]{1,0:T(8,128)(2,1)} %get-tuple-element.46), channel_id=1, source_target_pairs={{0,24},{4,28},{8,16},{12,20},{16,8},{20,12},{24,0},{28,4},{1,25},{... | collective-permute-start | bytes 442376 | tf_op jit(solution)/shard_map/ppermute | solution.py:57
  162.3 13.3 %all-to-all-done.2.lat = bf16[8,4,16,1024]{3,2,1,0:T(8,128)(2,1)S(1)} async-done(((bf16[8,4,16,1024]{3,2,1,0:T(8,128)(2,1)}), bf16[8,4,16,1024]{3,2,1,0:T(8,128)(2,1)S(1)}, u32[]{:S(2)}, u32[]{:S(2)}) %all-to-all-start.2) | async-done | bytes 1048608 | tf_op jit(solution)/shard_map/all_to_all | solution.py:61
  175.6 1.1 reduce.1.refs_0_
  176.9 1.5 collective-permute-start.16
  178.9 4.0 %collective-permute-done.21.refs_5_ = bf16[144,512]{1,0:T(8,128)(2,1)} collective-permute-done((bf16[144,512]{1,0:T(8,128)(2,1)}, bf16[144,512]{1,0:T(8,128)(2,1)}, u32[]{:S(2)}, u32[]{:S(2)}) %collective-permute-start.21) | collective-permute-done | bytes 147488 | tf_op jit(solution)/shard_map/ppermute | solution.py:57
  182.9 4.2 %all-to-all-start.3 = ((bf16[8,4,16,256]{3,2,1,0:T(8,128)(2,1)}), bf16[8,4,16,256]{3,2,1,0:T(8,128)(2,1)S(1)}, u32[]{:S(2)}, u32[]{:S(2)}) async-start(bf16[8,4,16,256]{3,2,1,0:T(8,128)(2,1)} %get-tuple-element.36), calls=%async_computation.3 | async-start | bytes 524288 | tf_op jit(solution)/shard_map/all_to_all | solution.py:61
  187.2 1.9 collective-permute-done.18.refs_3_
  189.0 2.5 %scatter.1.refs_0_ = bf16[144,1024]{1,0:T(8,128)(2,1)S(1)} custom-call(s32[2]{0:T(128)S(1)} %copy-done.7, s32[8,64]{1,0:T(8,128)S(1)} %copy-done.5, bf16[144,512]{1,0:T(8,128)(2,1)S(1)} %get-tuple-element.38.refs_0_, bf16[144,512]{1,0:T(8,128)(2,1)S(1)} %collective-permute-done.16.refs_1_, bf16[144,512]{1,0:T(8,128)(2,1)S(1)} %collective-permute-done.17.refs_2_, ...), custom_call_target="tpu_custom_call" | custom-call | tf_op jit(solution)/shard_map/scatter/pallas_call | solution.py:35
  191.5 1.5 collective-permute-start.25
  193.1 5.2 %collective-permute-done.25.refs_2_ = bf16[144,1024]{1,0:T(8,128)(2,1)S(1)} collective-permute-done((bf16[144,1024]{1,0:T(8,128)(2,1)S(1)}, bf16[144,1024]{1,0:T(8,128)(2,1)S(1)}, u32[]{:S(2)}, u32[]{:S(2)}) %collective-permute-start.25) | collective-permute-done | bytes 294944 | tf_op jit(solution)/shard_map/ppermute | solution.py:57
  198.3 0.7 copy.33
  199.1 0.7 copy.31
  199.7 0.7 copy.32
  200.4 2.1 %assemble.1 = f32[576,1024]{1,0:T(8,128)} custom-call(s32[2]{0:T(128)S(1)} %copy-done.7, bf16[144,1024]{1,0:T(8,128)(2,1)S(1)} %scatter.1.refs_0_, bf16[144,1024]{1,0:T(8,128)(2,1)S(1)} %collective-permute-done.24.refs_1_, bf16[144,1024]{1,0:T(8,128)(2,1)S(1)} %collective-permute-done.25.refs_2_, bf16[144,1024]{1,0:T(8,128)(2,1)S(1)} %collective-permute-done.26.refs_3_), custom_call_target="tpu_custom_call" | custom-call | tf_op jit(solution)/shard_map/assemble/pallas_call | solution.py:35
  (82 shorter events, 3.1 us)
Async XLA Ops:
  0.6 7.6 %copy-start.8 = (s32[1,64]{1,0:T(1,128)S(1)}, s32[1,64]{1,0:T(1,128)}, u32[]{:S(2)}) copy-start(s32[1,64]{1,0:T(1,128)} %own.1) | copy-start | bytes 772
  0.6 7.6 %collective-permute-start.1 = (s32[1,64]{1,0:T(1,128)}, s32[1,64]{1,0:T(1,128)S(1)}, u32[]{:S(2)}, u32[]{:S(2)}) collective-permute-start(s32[1,64]{1,0:T(1,128)} %own.1), channel_id=1, source_target_pairs={{0,4},{4,0},{8,12},{12,8},{16,20},{20,16},{24,28},{28,24},{1,5},{5... | collective-permute-start | bytes 776 | tf_op jit(solution)/shard_map/ppermute | solution.py:57
  3.7 60.6 %copy-start.6 = (s32[2]{0:T(128)}, s32[2]{0:T(128)S(1)}, u32[]{:S(2)}) copy-start(s32[2]{0:T(128)S(1)} %pad_add_fusion.3.ids) | copy-start | bytes 28
  3.8 1.3 copy-start.1
  5.0 4.9 %copy-start.19 = (bf16[16,32,128]{2,1,0:T(8,128)(2,1)S(1)}, bf16[16,32,128]{2,1,0:T(8,128)(2,1)}, u32[]{:S(2)}) copy-start(bf16[16,32,128]{2,1,0:T(8,128)(2,1)} %param.13) | copy-start | bytes 393220
  5.0 4.9 %copy-start.20 = (bf16[16,32,128]{2,1,0:T(8,128)(2,1)S(1)}, bf16[16,32,128]{2,1,0:T(8,128)(2,1)}, u32[]{:S(2)}) copy-start(bf16[16,32,128]{2,1,0:T(8,128)(2,1)} %param.8) | copy-start | bytes 393220
  5.0 5.0 %copy-start.15 = (bf16[32,8192]{1,0:T(8,128)(2,1)S(1)}, bf16[32,8192]{1,0:T(8,128)(2,1)}, u32[]{:S(2)}) copy-start(bf16[32,8192]{1,0:T(8,128)(2,1)} %param.11) | copy-start | bytes 1572868
  5.6 15.9 %collective-permute-start = (bf16[144,1024]{1,0:T(8,128)(2,1)S(1)}, bf16[144,1024]{1,0:T(8,128)(2,1)S(1)}, u32[]{:S(2)}, u32[]{:S(2)}) collective-permute-start(bf16[144,1024]{1,0:T(8,128)(2,1)S(1)} %cut.1.refs_0_), channel_id=1, source_target_pairs={{0,16},{4,20},{8,24},{12,28},{16,0},{20,4},{24,8},{28,12},{1,17},{... | collective-permute-start | bytes 884744 | tf_op jit(solution)/shard_map/ppermute | solution.py:57
  8.3 2.2 %copy-start.16 = (bf16[32,8192]{1,0:T(8,128)(2,1)S(1)}, bf16[32,8192]{1,0:T(8,128)(2,1)}, u32[]{:S(2)}) copy-start(bf16[32,8192]{1,0:T(8,128)(2,1)} %param.12) | copy-start | bytes 1572868
  8.3 6.0 %collective-permute-start.2 = (s32[2,64]{1,0:T(2,128)S(1)}, s32[2,64]{1,0:T(2,128)S(1)}, u32[]{:S(2)}, u32[]{:S(2)}) collective-permute-start(s32[2,64]{1,0:T(2,128)S(1)} %pad_add_fusion.2), channel_id=1, source_target_pairs={{0,8},{4,12},{8,0},{12,4},{16,24},{20,28},{24,16},{28,20},{1,9},{5... | collective-permute-start | bytes 1544 | tf_op jit(solution)/shard_map/ppermute | solution.py:57
  14.3 7.1 %collective-permute-start.3 = (s32[4,64]{1,0:T(4,128)S(1)}, s32[4,64]{1,0:T(4,128)S(1)}, u32[]{:S(2)}, u32[]{:S(2)}) collective-permute-start(s32[4,64]{1,0:T(4,128)S(1)} %pad_add_fusion.1), channel_id=1, source_target_pairs={{0,16},{4,20},{8,24},{12,28},{16,0},{20,4},{24,8},{28,12},{1,17},{... | collective-permute-start | bytes 3080 | tf_op jit(solution)/shard_map/ppermute | solution.py:57
  22.1 36.4 %all-to-all-start = ((bf16[32,160,128]{2,1,0:T(8,128)(2,1)}), bf16[32,160,128]{2,1,0:T(8,128)(2,1)S(1)}, u32[]{:S(2)}, u32[]{:S(2)}) async-start(bf16[32,160,128]{2,1,0:T(8,128)(2,1)} %after.1), calls=%async_computation | async-start | bytes 2621440 | tf_op jit(solution)/shard_map/all_to_all | solution.py:61
  26.8 37.5 %collective-permute-start.4 = (bf16[144,1024]{1,0:T(8,128)(2,1)S(1)}, bf16[144,1024]{1,0:T(8,128)(2,1)S(1)}, u32[]{:S(2)}, u32[]{:S(2)}) collective-permute-start(bf16[144,1024]{1,0:T(8,128)(2,1)S(1)} %cut.1.refs_0_), channel_id=1, source_target_pairs={{0,8},{4,12},{8,0},{12,4},{16,24},{20,28},{24,16},{28,20},{1,9},{5... | collective-permute-start | bytes 884744 | tf_op jit(solution)/shard_map/ppermute | solution.py:57
  28.8 35.5 %collective-permute-start.5 = (bf16[144,1024]{1,0:T(8,128)(2,1)S(1)}, bf16[144,1024]{1,0:T(8,128)(2,1)S(1)}, u32[]{:S(2)}, u32[]{:S(2)}) collective-permute-start(bf16[144,1024]{1,0:T(8,128)(2,1)S(1)} %collective-permute-done.refs_1_.refs_2_), channel_id=1, source_target_pairs={{0,8},{4,12},{8,0},{12,4},{16,24},{20,28},{24,16},{28,20},{1,9},{5... | collective-permute-start | bytes 884744 | tf_op jit(solution)/shard_map/ppermute | solution.py:57
  59.9 45.0 %copy-start.17 = (bf16[16,32,64]{2,1,0:T(8,128)(2,1)S(1)}, bf16[16,32,64]{2,1,0:T(8,128)(2,1)}, u32[]{:S(2)}) copy-start(bf16[16,32,64]{2,1,0:T(8,128)(2,1)} %param.9) | copy-start | bytes 196612
  59.9 47.8 %all-to-all-start.1 = ((bf16[8,4,16,1024]{3,2,1,0:T(8,128)(2,1)}), bf16[8,4,16,1024]{3,2,1,0:T(8,128)(2,1)}, u32[]{:S(2)}, u32[]{:S(2)}) async-start(bf16[8,4,16,1024]{3,2,1,0:T(8,128)(2,1)} %expand.1), calls=%async_computation.1 | async-start | bytes 2097152 | tf_op jit(solution)/shard_map/all_to_all | solution.py:61
  67.6 40.0 %copy-start.3 = (bf16[144,2048]{1,0:T(8,128)(2,1)}, bf16[144,2048]{1,0:T(8,128)(2,1)S(1)}, u32[]{:S(2)}) copy-start(bf16[144,2048]{1,0:T(8,128)(2,1)S(1)} %get-tuple-element.26.refs_0_) | copy-start | bytes 1769476
  67.6 22.7 %collective-permute-start.9 = (bf16[144,2048]{1,0:T(8,128)(2,1)S(1)}, bf16[144,2048]{1,0:T(8,128)(2,1)S(1)}, u32[]{:S(2)}, u32[]{:S(2)}) collective-permute-start(bf16[144,2048]{1,0:T(8,128)(2,1)S(1)} %get-tuple-element.27), channel_id=1, source_target_pairs={{0,4},{4,0},{8,12},{12,8},{16,20},{20,16},{24,28},{28,24},{1,5},{5... | collective-permute-start | bytes 1769480 | tf_op jit(solution)/shard_map/ppermute | solution.py:57
  69.6 22.8 %collective-permute-start.7 = (bf16[144,2048]{1,0:T(8,128)(2,1)S(1)}, bf16[144,2048]{1,0:T(8,128)(2,1)S(1)}, u32[]{:S(2)}, u32[]{:S(2)}) collective-permute-start(bf16[144,2048]{1,0:T(8,128)(2,1)S(1)} %get-tuple-element.26.refs_0_), channel_id=1, source_target_pairs={{0,2},{1,3},{2,0},{3,1},{4,6},{5,7},{6,4},{7,5},{8,10},{9,11},{10,... | collective-permute-start | bytes 1769480 | tf_op jit(solution)/shard_map/ppermute | solution.py:57
  90.4 17.3 %copy-start.9 = (bf16[144,2048]{1,0:T(8,128)(2,1)}, bf16[144,2048]{1,0:T(8,128)(2,1)S(1)}, u32[]{:S(2)}) copy-start(bf16[144,2048]{1,0:T(8,128)(2,1)S(1)} %collective-permute-done.9.refs_4_) | copy-start | bytes 1769476
  90.4 14.5 %collective-permute-start.11 = (bf16[144,2048]{1,0:T(8,128)(2,1)S(1)}, bf16[144,2048]{1,0:T(8,128)(2,1)S(1)}, u32[]{:S(2)}, u32[]{:S(2)}) collective-permute-start(bf16[144,2048]{1,0:T(8,128)(2,1)S(1)} %collective-permute-done.9.refs_4_), channel_id=1, source_target_pairs={{0,2},{1,3},{2,0},{3,1},{4,6},{5,7},{6,4},{7,5},{8,10},{9,11},{10,... | collective-permute-start | bytes 1769480 | tf_op jit(solution)/shard_map/ppermute | solution.py:57
  91.9 13.9 %collective-permute-start.6 = (bf16[144,2048]{1,0:T(8,128)(2,1)S(1)}, bf16[144,2048]{1,0:T(8,128)(2,1)S(1)}, u32[]{:S(2)}, u32[]{:S(2)}) collective-permute-start(bf16[144,2048]{1,0:T(8,128)(2,1)S(1)} %get-tuple-element.26.refs_0_), channel_id=1, source_target_pairs={{0,1},{1,0},{2,3},{3,2},{4,5},{5,4},{6,7},{7,6},{8,9},{9,8},{10,11... | collective-permute-start | bytes 1769480 | tf_op jit(solution)/shard_map/ppermute | solution.py:57
  91.9 13.9 %collective-permute-start.10 = (bf16[144,2048]{1,0:T(8,128)(2,1)S(1)}, bf16[144,2048]{1,0:T(8,128)(2,1)S(1)}, u32[]{:S(2)}, u32[]{:S(2)}) collective-permute-start(bf16[144,2048]{1,0:T(8,128)(2,1)S(1)} %collective-permute-done.9.refs_4_), channel_id=1, source_target_pairs={{0,1},{1,0},{2,3},{3,2},{4,5},{5,4},{6,7},{7,6},{8,9},{9,8},{10,11... | collective-permute-start | bytes 1769480 | tf_op jit(solution)/shard_map/ppermute | solution.py:57
  92.4 15.3 %copy-start.10 = (bf16[144,2048]{1,0:T(8,128)(2,1)}, bf16[144,2048]{1,0:T(8,128)(2,1)S(1)}, u32[]{:S(2)}) copy-start(bf16[144,2048]{1,0:T(8,128)(2,1)S(1)} %collective-permute-done.7.refs_2_) | copy-start | bytes 1769476
  92.4 13.4 %collective-permute-start.8 = (bf16[144,2048]{1,0:T(8,128)(2,1)S(1)}, bf16[144,2048]{1,0:T(8,128)(2,1)S(1)}, u32[]{:S(2)}, u32[]{:S(2)}) collective-permute-start(bf16[144,2048]{1,0:T(8,128)(2,1)S(1)} %collective-permute-done.7.refs_2_), channel_id=1, source_target_pairs={{0,1},{1,0},{2,3},{3,2},{4,5},{5,4},{6,7},{7,6},{8,9},{9,8},{10,11... | collective-permute-start | bytes 1769480 | tf_op jit(solution)/shard_map/ppermute | solution.py:57
  104.9 2.7 %collective-permute-start.12 = (bf16[144,2048]{1,0:T(8,128)(2,1)S(1)}, bf16[144,2048]{1,0:T(8,128)(2,1)}, u32[]{:S(2)}, u32[]{:S(2)}) collective-permute-start(bf16[144,2048]{1,0:T(8,128)(2,1)S(1)} %collective-permute-done.11.refs_6_), channel_id=1, source_target_pairs={{0,1},{1,0},{2,3},{3,2},{4,5},{5,4},{6,7},{7,6},{8,9},{9,8},{10,11... | collective-permute-start | bytes 1769480 | tf_op jit(solution)/shard_map/ppermute | solution.py:57
  105.7 1.0 copy-start.13
  130.8 5.2 %copy-start = (bf16[2,144,2048]{2,1,0:T(8,128)(2,1)S(1)}, bf16[2,144,2048]{2,1,0:T(8,128)(2,1)}, u32[]{:S(2)}) copy-start(bf16[2,144,2048]{2,1,0:T(8,128)(2,1)} %get-tuple-element.29.keep) | copy-start | bytes 3538948
  130.8 5.2 %collective-permute-start.13 = (bf16[2,144,2048]{2,1,0:T(8,128)(2,1)}, bf16[2,144,2048]{2,1,0:T(8,128)(2,1)}, u32[]{:S(2)}, u32[]{:S(2)}) collective-permute-start(bf16[2,144,2048]{2,1,0:T(8,128)(2,1)} %get-tuple-element.30), channel_id=1, source_target_pairs={{0,1},{1,0},{2,3},{3,2},{4,5},{5,4},{6,7},{7,6},{8,9},{9,8},{10,11... | collective-permute-start | bytes 3538952 | tf_op jit(solution)/shard_map/ppermute | solution.py:57
  131.3 44.4 %all-to-all-start.2 = ((bf16[8,4,16,1024]{3,2,1,0:T(8,128)(2,1)}), bf16[8,4,16,1024]{3,2,1,0:T(8,128)(2,1)S(1)}, u32[]{:S(2)}, u32[]{:S(2)}) async-start(bf16[8,4,16,1024]{3,2,1,0:T(8,128)(2,1)} %bitcast.36), calls=%async_computation.2 | async-start | bytes 2097152 | tf_op jit(solution)/shard_map/all_to_all | solution.py:61
  135.9 3.3 %copy-start.2 = (bf16[2,144,2048]{2,1,0:T(8,128)(2,1)S(1)}, bf16[2,144,2048]{2,1,0:T(8,128)(2,1)}, u32[]{:S(2)}) copy-start(bf16[2,144,2048]{2,1,0:T(8,128)(2,1)} %get-tuple-element.32.refs_1_) | copy-start | bytes 3538948
  135.9 3.3 %collective-permute-start.14 = (bf16[2,144,2048]{2,1,0:T(8,128)(2,1)}, bf16[2,144,2048]{2,1,0:T(8,128)(2,1)S(1)}, u32[]{:S(2)}, u32[]{:S(2)}) collective-permute-start(bf16[2,144,2048]{2,1,0:T(8,128)(2,1)} %get-tuple-element.33), channel_id=1, source_target_pairs={{0,1},{1,0},{2,3},{3,2},{4,5},{5,4},{6,7},{7,6},{8,9},{9,8},{10,11... | collective-permute-start | bytes 3538952 | tf_op jit(solution)/shard_map/ppermute | solution.py:57
  137.6 16.2 %collective-permute-start.19 = (bf16[144,2048]{1,0:T(8,128)(2,1)S(1)}, bf16[144,2048]{1,0:T(8,128)(2,1)S(1)}, u32[]{:S(2)}, u32[]{:S(2)}) collective-permute-start(bf16[144,2048]{1,0:T(8,128)(2,1)S(1)} %get-tuple-element.43), channel_id=1, source_target_pairs={{0,2},{1,3},{2,0},{3,1},{4,6},{5,7},{6,4},{7,5},{8,10},{9,11},{10,... | collective-permute-start | bytes 1769480 | tf_op jit(solution)/shard_map/ppermute | solution.py:57
  140.1 36.6 %collective-permute-start.15 = (bf16[144,2048]{1,0:T(8,128)(2,1)}, bf16[144,2048]{1,0:T(8,128)(2,1)S(1)}, u32[]{:S(2)}, u32[]{:S(2)}) collective-permute-start(bf16[144,2048]{1,0:T(8,128)(2,1)} %get-tuple-element.35), channel_id=1, source_target_pairs={{0,2},{1,3},{2,0},{3,1},{4,6},{5,7},{6,4},{7,5},{8,10},{9,11},{10,... | collective-permute-start | bytes 1769480 | tf_op jit(solution)/shard_map/ppermute | solution.py:57
  154.7 24.2 %collective-permute-start.20 = (bf16[144,512]{1,0:T(8,128)(2,1)}, bf16[144,512]{1,0:T(8,128)(2,1)}, u32[]{:S(2)}, u32[]{:S(2)}) collective-permute-start(bf16[144,512]{1,0:T(8,128)(2,1)} %get-tuple-element.44), channel_id=1, source_target_pairs={{0,16},{4,20},{8,24},{12,28},{16,0},{20,4},{24,8},{28,12},{1,17},{... | collective-permute-start | bytes 442376 | tf_op jit(solution)/shard_map/ppermute | solution.py:57
  157.5 25.4 %collective-permute-start.21 = (bf16[144,512]{1,0:T(8,128)(2,1)}, bf16[144,512]{1,0:T(8,128)(2,1)}, u32[]{:S(2)}, u32[]{:S(2)}) collective-permute-start(bf16[144,512]{1,0:T(8,128)(2,1)} %get-tuple-element.45), channel_id=1, source_target_pairs={{0,20},{4,16},{8,28},{12,24},{16,4},{20,0},{24,12},{28,8},{1,21},{... | collective-permute-start | bytes 442376 | tf_op jit(solution)/shard_map/ppermute | solution.py:57
  159.0 28.1 %collective-permute-start.22 = (bf16[144,512]{1,0:T(8,128)(2,1)}, bf16[144,512]{1,0:T(8,128)(2,1)}, u32[]{:S(2)}, u32[]{:S(2)}) collective-permute-start(bf16[144,512]{1,0:T(8,128)(2,1)} %get-tuple-element.46), channel_id=1, source_target_pairs={{0,24},{4,28},{8,16},{12,20},{16,8},{20,12},{24,0},{28,4},{1,25},{... | collective-permute-start | bytes 442376 | tf_op jit(solution)/shard_map/ppermute | solution.py:57
  162.2 24.9 %collective-permute-start.23 = (bf16[144,512]{1,0:T(8,128)(2,1)}, bf16[144,512]{1,0:T(8,128)(2,1)}, u32[]{:S(2)}, u32[]{:S(2)}) collective-permute-start(bf16[144,512]{1,0:T(8,128)(2,1)} %get-tuple-element.47), channel_id=1, source_target_pairs={{0,28},{4,24},{8,20},{12,16},{16,12},{20,8},{24,4},{28,0},{1,29},{... | collective-permute-start | bytes 442376 | tf_op jit(solution)/shard_map/ppermute | solution.py:57
  176.8 12.3 %copy-start.5 = (s32[8,64]{1,0:T(8,128)S(1)}, s32[8,64]{1,0:T(8,128)}, u32[]{:S(2)}) copy-start(s32[8,64]{1,0:T(8,128)} %copy-done.4) | copy-start | bytes 6148
  176.8 12.3 %copy-start.7 = (s32[2]{0:T(128)S(1)}, s32[2]{0:T(128)}, u32[]{:S(2)}) copy-start(s32[2]{0:T(128)} %copy-done.6) | copy-start | bytes 28
  176.9 21.4 %copy-start.18 = (bf16[512,64]{1,0:T(8,128)(2,1)S(1)}, bf16[512,64]{1,0:T(8,128)(2,1)}, u32[]{:S(2)}) copy-start(bf16[512,64]{1,0:T(8,128)(2,1)} %get-tuple-element.37) | copy-start | bytes 196612
  176.9 10.2 %collective-permute-start.16 = (bf16[144,512]{1,0:T(8,128)(2,1)S(1)}, bf16[144,512]{1,0:T(8,128)(2,1)S(1)}, u32[]{:S(2)}, u32[]{:S(2)}) collective-permute-start(bf16[144,512]{1,0:T(8,128)(2,1)S(1)} %get-tuple-element.39), channel_id=1, source_target_pairs={{0,4},{4,0},{8,12},{12,8},{16,20},{20,16},{24,28},{28,24},{1,5},{5... | collective-permute-start | bytes 442376 | tf_op jit(solution)/shard_map/ppermute | solution.py:57
  178.9 8.3 %collective-permute-start.17 = (bf16[144,512]{1,0:T(8,128)(2,1)S(1)}, bf16[144,512]{1,0:T(8,128)(2,1)S(1)}, u32[]{:S(2)}, u32[]{:S(2)}) collective-permute-start(bf16[144,512]{1,0:T(8,128)(2,1)S(1)} %get-tuple-element.40), channel_id=1, source_target_pairs={{0,8},{4,12},{8,0},{12,4},{16,24},{20,28},{24,16},{28,20},{1,9},{5... | collective-permute-start | bytes 442376 | tf_op jit(solution)/shard_map/ppermute | solution.py:57
  182.9 6.1 %collective-permute-start.18 = (bf16[144,512]{1,0:T(8,128)(2,1)S(1)}, bf16[144,512]{1,0:T(8,128)(2,1)S(1)}, u32[]{:S(2)}, u32[]{:S(2)}) collective-permute-start(bf16[144,512]{1,0:T(8,128)(2,1)S(1)} %get-tuple-element.41), channel_id=1, source_target_pairs={{0,12},{4,8},{8,4},{12,0},{16,28},{20,24},{24,20},{28,16},{1,13},{... | collective-permute-start | bytes 442376 | tf_op jit(solution)/shard_map/ppermute | solution.py:57
  182.9 16.1 %all-to-all-start.3 = ((bf16[8,4,16,256]{3,2,1,0:T(8,128)(2,1)}), bf16[8,4,16,256]{3,2,1,0:T(8,128)(2,1)S(1)}, u32[]{:S(2)}, u32[]{:S(2)}) async-start(bf16[8,4,16,256]{3,2,1,0:T(8,128)(2,1)} %get-tuple-element.36), calls=%async_computation.3 | async-start | bytes 524288 | tf_op jit(solution)/shard_map/all_to_all | solution.py:61
  191.5 6.8 %collective-permute-start.25 = (bf16[144,1024]{1,0:T(8,128)(2,1)S(1)}, bf16[144,1024]{1,0:T(8,128)(2,1)S(1)}, u32[]{:S(2)}, u32[]{:S(2)}) collective-permute-start(bf16[144,1024]{1,0:T(8,128)(2,1)S(1)} %scatter.1.refs_0_), channel_id=1, source_target_pairs={{0,2},{1,3},{2,0},{3,1},{4,6},{5,7},{6,4},{7,5},{8,10},{9,11},{10,... | collective-permute-start | bytes 884744 | tf_op jit(solution)/shard_map/ppermute | solution.py:57
  193.1 7.4 %collective-permute-start.24 = (bf16[144,1024]{1,0:T(8,128)(2,1)S(1)}, bf16[144,1024]{1,0:T(8,128)(2,1)S(1)}, u32[]{:S(2)}, u32[]{:S(2)}) collective-permute-start(bf16[144,1024]{1,0:T(8,128)(2,1)S(1)} %scatter.1.refs_0_), channel_id=1, source_target_pairs={{0,1},{1,0},{2,3},{3,2},{4,5},{5,4},{6,7},{7,6},{8,9},{9,8},{10,11... | collective-permute-start | bytes 884744 | tf_op jit(solution)/shard_map/ppermute | solution.py:57
  198.3 2.1 %collective-permute-start.26 = (bf16[144,1024]{1,0:T(8,128)(2,1)S(1)}, bf16[144,1024]{1,0:T(8,128)(2,1)S(1)}, u32[]{:S(2)}, u32[]{:S(2)}) collective-permute-start(bf16[144,1024]{1,0:T(8,128)(2,1)S(1)} %collective-permute-done.25.refs_2_), channel_id=1, source_target_pairs={{0,1},{1,0},{2,3},{3,2},{4,5},{5,4},{6,7},{7,6},{8,9},{9,8},{10,11... | collective-permute-start | bytes 884744 | tf_op jit(solution)/shard_map/ppermute | solution.py:57
  (4 other events, 3.2 us)

commit v3 on v2

--- a/solution.py
+++ b/solution.py
@@ -75,8 +75,8 @@
 
 
 def gather_kernel(per_peer, ids, own, other, *refs):
-    owners = len(refs) - 2
-    caches, outs = refs[:owners], refs[owners:]
+    owners = len(refs) - 3
+    caches, outs = refs[:owners], refs[owners + 1 :]
     lanes = per_peer * BLOCK_LEN
 
     def block(row, i, j):
@@ -135,7 +135,7 @@
     return jnp.concatenate([pack[r, head, start : start + rows, :] for r in range(peers)], axis=0)
 
 
-def expand_kernel(sizes, pack, out):
+def expand_kernel(sizes, pack, away, asked, out):
     uk_rows, uv_rows, queries, tiles, latent = sizes
     peers, heads = pack.shape[0], pack.shape[1]
     for h in range(heads):
@@ -177,7 +177,7 @@
 
 
 def attend_kernel(scale, per_peer, ids, sel, rope, qd, *refs):
-    keys, refs = (refs[:4], refs[4:8]), refs[9:]
+    keys, refs = (refs[:4], refs[4:8]), refs[8:]
     keeps, sends, lat, d_rope, refs = (refs[0], refs[2]), (refs[1], refs[3]), refs[4], refs[5], refs[6:]
     kt_near, kt_far, pb_near, pb_far, qx, do, sc, flip, cat, o_full, dq = refs
     rows, latent = do.shape
@@ -295,9 +295,9 @@
     (c0,) = call(cut_kernel, "cut", (ids, cache.T), [SMEM, VMEM], [((depth, tokens), BF16)])
     c2 = swap(c0, "seq", 4)
     c1 = swap(c0, "seq", 2)
-    asked = jnp.concatenate([slot_blocks, row1], axis=0)
-    for bit in (2, 4):
-        asked = jnp.concatenate([asked, swap(asked, "seq", bit)], axis=0)
+    asked_y = jnp.concatenate([slot_blocks, row1], axis=0)
+    asked_z = jnp.concatenate([asked_y, swap(asked_y, "seq", 2)], axis=0)
+    asked = jnp.concatenate([asked_z, swap(asked_z, "seq", 4)], axis=0)
 
     n_rows = w_uk.shape[1] // latent
     l_rows = w_uv.shape[1] // value
@@ -312,26 +312,26 @@
         ],
         axis=1,
     )
-    (pack,) = call(tie_kernel, "after", (c2, asked), [ANY] * 2, [], tied=pack)
+    (pack,) = call(tie_kernel, "after", (c2,), [ANY], [], tied=pack)
     pack = seq_swap(pack).reshape(peers, share, -1, LANES)
+    c3 = swap(c2, "seq", 2)
+    away, k0 = call(
+        functools.partial(gather_kernel, per_peer),
+        "gather",
+        (ids, slot_blocks, row1, c0, c1, c2, c3, asked_z),
+        [SMEM] * 3 + [VMEM] * 4 + [ANY],
+        [((depth, half), BF16)] * 2,
+    )
     sizes = (n_rows * tiles, l_rows, queries, tiles, latent)
     (lat,) = call(
         functools.partial(expand_kernel, sizes),
         "expand",
-        (pack,),
-        [VMEM],
+        (pack, away, asked),
+        [VMEM, ANY, ANY],
         [((peers, share, queries, 2 * latent), BF16)],
     )
     qd = seq_swap(lat).reshape(rows, 2 * latent)
 
-    c3 = swap(c2, "seq", 2)
-    away, k0 = call(
-        functools.partial(gather_kernel, per_peer),
-        "gather",
-        (ids, slot_blocks, row1, c0, c1, c2, c3),
-        [SMEM] * 3 + [VMEM] * 4,
-        [((depth, half), BF16)] * 2,
-    )
     keys = []
     for k in (k0, swap(away, "seq", 1)):
         k2 = swap(k, "grp", 2)
@@ -340,8 +340,8 @@
     near_keep, near_send, far_keep, far_send, lat, d_rope = call(
         functools.partial(attend_kernel, scale, per_peer),
         "attend",
-        (ids, sel, rope_rows, qd, *keys, asked),
-        [SMEM] + [VMEM] * 11 + [ANY],
+        (ids, sel, rope_rows, qd, *keys),
+        [SMEM] + [VMEM] * 11,
         [((2, depth, half), BF16)] * 4 + [((rows, 2 * latent), BF16), ((rows, rope), BF16)],
         [pltpu.VMEM((width + slots, half), BF16)] * 2
         + [pltpu.VMEM((rows, half), BF16)] * 2
@@ -377,7 +377,8 @@
         [VMEM] * 2,
         [((peers, share, queries, value + nope), BF16)],
     )
-    res, *near = owner(*near, tied=res)
+    near = owner(*near)
+    (res,) = call(tie_kernel, "after", (near[0],), [ANY], [], tied=res)
     got = exchange([*near, *far])
     res = seq_swap(res).reshape(heads, queries, value + nope)
 

time: 204 us -> 213 us (1.044)
  waiting for transfers between devices: 106 us -> 111 us
  starting transfers between devices: 49.4 us -> 54.2 us
    ppermute x27, waiting for transfers between devices: 63 us -> 111 us  [swap(): return lax.ppermute(x, axis, [(i, i ^ bit) for i in range(n)])]
    all_to_all x4, waiting for transfers between devices: 42.9 us -> 0.01 us  [seq_swap(): return lax.all_to_all(x, 'seq', split_axis=0, concat_axis=0, tiled=True)]
    all_to_all x4, starting transfers between devices: 17.9 us -> 20.7 us  [seq_swap(): return lax.all_to_all(x, 'seq', split_axis=0, concat_axis=0, tiled=True)]
    pallas_call x12 -> x13, Pallas kernels: 37.7 us -> 37.2 us  [call(): pl.pallas_call(body, out_shape=out_shape, in_specs=specs, out_specs=out_s...]
    unnamed x46 -> x42, local copies, waits for them, and re-layouts: 6.07 us -> 6.21 us
  transfers between devices with their start and end apart: 31 -> 31, of which waited for: 11 -> 12; matrix products, arithmetic and copies ran while one was open for 2% -> 2% of each run, Pallas kernels for 6% -> 5%
where the time goes in v3:
time: 213 us; the launch traced here: 212 us
  waiting for transfers between devices  111 us (52%)
  starting transfers between devices  54.2 us (25%)
  Pallas kernels  37.2 us (17%)
  local copies, waits for them, and re-layouts  7.51 us (4%)
    ppermute x27, waiting for transfers between devices, swap(): return lax.ppermute(x, axis, [(i, i ^ bit) for i in range(n)])  111 us
    pallas_call x13, Pallas kernels, call(): pl.pallas_call(body, out_shape=out_shape, in_specs=specs, out_specs=out_s...  37.2 us
    ppermute x27, starting transfers between devices, swap(): return lax.ppermute(x, axis, [(i, i ^ bit) for i in range(n)])  33.5 us
    all_to_all x4, starting transfers between devices, seq_swap(): return lax.all_to_all(x, 'seq', split_axis=0, concat_axis=0, tiled=True)  20.7 us
    unnamed x42, local copies, waits for them, and re-layouts  6.21 us
  transfers between devices with their start and end apart: 31, of which 12 were waited for; matrix products, arithmetic and copies ran while one was open for 2% of the time, Pallas kernels for 5%

profile of v3, /device:TPU:0, one launch (start us, length us, event | category | flops | bytes accessed | tf_op | source)
XLA Modules:
  0.0 211.8 jit_solution(1151407472627554957)
XLA Ops:
  0.7 1.3 copy-done.1
  2.6 4.1 %collective-permute-start = (bf16[144,1024]{1,0:T(8,128)(2,1)S(1)}, bf16[144,1024]{1,0:T(8,128)(2,1)S(1)}, u32[]{:S(2)}, u32[]{:S(2)}) collective-permute-start(bf16[144,1024]{1,0:T(8,128)(2,1)S(1)} %cut.1.refs_0_), channel_id=1, source_target_pairs={{0,16},{4,20},{8,24},{12,28},{16,0},{20,4},{24,8},{28,12},{1,17},{... | collective-permute-start | bytes 884744 | tf_op jit(solution)/shard_map/ppermute | solution.py:57
  8.1 1.1 pad_maximum_fusion.refs_0_
  9.3 10.7 %collective-permute-done.refs_1_.refs_2_ = bf16[144,1024]{1,0:T(8,128)(2,1)S(1)} collective-permute-done((bf16[144,1024]{1,0:T(8,128)(2,1)S(1)}, bf16[144,1024]{1,0:T(8,128)(2,1)S(1)}, u32[]{:S(2)}, u32[]{:S(2)}) %collective-permute-start) | collective-permute-done | bytes 294944 | tf_op jit(solution)/shard_map/ppermute | solution.py:57
  20.0 5.9 %all-to-all-start = ((bf16[32,160,128]{2,1,0:T(8,128)(2,1)}), bf16[32,160,128]{2,1,0:T(8,128)(2,1)S(1)}, u32[]{:S(2)}, u32[]{:S(2)}) async-start(bf16[32,160,128]{2,1,0:T(8,128)(2,1)} %after.2), calls=%async_computation | async-start | bytes 2621440 | tf_op jit(solution)/shard_map/all_to_all | solution.py:61
  25.9 2.0 collective-permute-start.1
  27.9 1.5 collective-permute-start.2
  30.0 6.0 %collective-permute-done.1.other = s32[1,64]{1,0:T(1,128)S(1)} collective-permute-done((s32[1,64]{1,0:T(1,128)S(1)}, s32[1,64]{1,0:T(1,128)S(1)}, u32[]{:S(2)}, u32[]{:S(2)}) %collective-permute-start.1) | collective-permute-done | bytes 288 | tf_op jit(solution)/shard_map/ppermute | solution.py:57
  36.0 2.7 %collective-permute-start.4 = (s32[2,64]{1,0:T(2,128)S(1)}, s32[2,64]{1,0:T(2,128)S(1)}, u32[]{:S(2)}, u32[]{:S(2)}) collective-permute-start(s32[2,64]{1,0:T(2,128)S(1)} %pad_add_fusion.2), channel_id=1, source_target_pairs={{0,8},{4,12},{8,0},{12,4},{16,24},{20,28},{24,16},{28,20},{1,9},{5... | collective-permute-start | bytes 1544 | tf_op jit(solution)/shard_map/ppermute | solution.py:57
  38.6 23.6 %collective-permute-done.4 = s32[2,64]{1,0:T(2,128)S(1)} collective-permute-done((s32[2,64]{1,0:T(2,128)S(1)}, s32[2,64]{1,0:T(2,128)S(1)}, u32[]{:S(2)}, u32[]{:S(2)}) %collective-permute-start.4) | collective-permute-done | bytes 544 | tf_op jit(solution)/shard_map/ppermute | solution.py:57
  62.3 2.5 %collective-permute-start.5 = (s32[4,64]{1,0:T(4,128)S(1)}, s32[4,64]{1,0:T(4,128)S(1)}, u32[]{:S(2)}, u32[]{:S(2)}) collective-permute-start(s32[4,64]{1,0:T(4,128)S(1)} %pad_add_fusion.1.refs_4_), channel_id=1, source_target_pairs={{0,16},{4,20},{8,24},{12,28},{16,0},{20,4},{24,8},{28,12},{1,17},{... | collective-permute-start | bytes 3080 | tf_op jit(solution)/shard_map/ppermute | solution.py:57
  64.8 2.0 collective-permute-done.5
  66.9 3.3 %gather.1 = (bf16[144,2048]{1,0:T(8,128)(2,1)S(1)}, bf16[144,2048]{1,0:T(8,128)(2,1)S(1)}) custom-call(s32[2]{0:T(128)S(1)} %pad_add_fusion.3.ids, s32[1,64]{1,0:T(1,128)S(1)} %copy-done.6, s32[1,64]{1,0:T(1,128)S(1)} %collective-permute-done.1.other, bf16[144,1024]{1,0:T(8,128)(2,1)S(1)} %cut.1.refs_0_, ...), custom_call_target="tpu_custom_call" | custom-call | tf_op jit(solution)/shard_map/gather/pallas_call | solution.py:35
  70.2 1.4 expand.1
  71.6 4.8 %all-to-all-start.1 = ((bf16[8,4,16,1024]{3,2,1,0:T(8,128)(2,1)}), bf16[8,4,16,1024]{3,2,1,0:T(8,128)(2,1)}, u32[]{:S(2)}, u32[]{:S(2)}) async-start(bf16[8,4,16,1024]{3,2,1,0:T(8,128)(2,1)} %expand.1), calls=%async_computation.1 | async-start | bytes 2097152 | tf_op jit(solution)/shard_map/all_to_all | solution.py:61
  76.4 2.0 collective-permute-start.9
  78.4 1.5 collective-permute-start.7
  79.9 20.6 %collective-permute-done.9.refs_4_ = bf16[144,2048]{1,0:T(8,128)(2,1)S(1)} collective-permute-done((bf16[144,2048]{1,0:T(8,128)(2,1)S(1)}, bf16[144,2048]{1,0:T(8,128)(2,1)S(1)}, u32[]{:S(2)}, u32[]{:S(2)}) %collective-permute-start.9) | collective-permute-done | bytes 589856 | tf_op jit(solution)/shard_map/ppermute | solution.py:57
  100.5 1.5 collective-permute-start.11
  102.5 10.9 %collective-permute-done.11.refs_6_ = bf16[144,2048]{1,0:T(8,128)(2,1)S(1)} collective-permute-done((bf16[144,2048]{1,0:T(8,128)(2,1)S(1)}, bf16[144,2048]{1,0:T(8,128)(2,1)S(1)}, u32[]{:S(2)}, u32[]{:S(2)}) %collective-permute-start.11) | collective-permute-done | bytes 589856 | tf_op jit(solution)/shard_map/ppermute | solution.py:57
  113.4 0.8 copy.34
  114.3 0.8 copy-done.10
  115.3 0.9 copy-done.12
  116.2 23.2 %attend.1 = (bf16[2,144,2048]{2,1,0:T(8,128)(2,1)}, bf16[2,144,2048]{2,1,0:T(8,128)(2,1)}, bf16[2,144,2048]{2,1,0:T(8,128)(2,1)}, bf16[2,144,2048]{2,1,0:T(8,128...) custom-call(s32[2]{0:T(128)} %copy-done.4, s32[16,32]{1,0:T(8,128)} %sel.1, bf16[32,16,64]{2,1,0:T(8,128)(2,1)} %bitcast.38, ...), custom_call_target="tpu_custom_call" | custom-call | tf_op jit(solution)/shard_map/attend/pallas_call | solution.py:35
  139.8 5.7 %all-to-all-start.2 = ((bf16[8,4,16,1024]{3,2,1,0:T(8,128)(2,1)}), bf16[8,4,16,1024]{3,2,1,0:T(8,128)(2,1)S(1)}, u32[]{:S(2)}, u32[]{:S(2)}) async-start(bf16[8,4,16,1024]{3,2,1,0:T(8,128)(2,1)} %bitcast.36), calls=%async_computation.2 | async-start | bytes 2097152 | tf_op jit(solution)/shard_map/all_to_all | solution.py:61
  145.7 1.7 pair.2
  147.4 1.5 collective-permute-start.19
  149.2 1.3 collective-permute-start.15
  150.5 13.1 %collective-permute-done.19.got = bf16[144,2048]{1,0:T(8,128)(2,1)S(1)} collective-permute-done((bf16[144,2048]{1,0:T(8,128)(2,1)S(1)}, bf16[144,2048]{1,0:T(8,128)(2,1)S(1)}, u32[]{:S(2)}, u32[]{:S(2)}) %collective-permute-start.19) | collective-permute-done | bytes 589856 | tf_op jit(solution)/shard_map/ppermute | solution.py:57
  163.6 0.8 owner.3
  164.4 2.9 %collective-permute-start.20 = (bf16[144,512]{1,0:T(8,128)(2,1)S(1)}, bf16[144,512]{1,0:T(8,128)(2,1)S(1)}, u32[]{:S(2)}, u32[]{:S(2)}) collective-permute-start(bf16[144,512]{1,0:T(8,128)(2,1)S(1)} %get-tuple-element.42), channel_id=1, source_target_pairs={{0,16},{4,20},{8,24},{12,28},{16,0},{20,4},{24,8},{28,12},{1,17},{... | collective-permute-start | bytes 442376 | tf_op jit(solution)/shard_map/ppermute | solution.py:57
  167.2 1.5 collective-permute-start.21
  168.7 3.3 %collective-permute-start.22 = (bf16[144,512]{1,0:T(8,128)(2,1)}, bf16[144,512]{1,0:T(8,128)(2,1)S(1)}, u32[]{:S(2)}, u32[]{:S(2)}) collective-permute-start(bf16[144,512]{1,0:T(8,128)(2,1)} %get-tuple-element.44), channel_id=1, source_target_pairs={{0,24},{4,28},{8,16},{12,20},{16,8},{20,12},{24,0},{28,4},{1,25},{... | collective-permute-start | bytes 442376 | tf_op jit(solution)/shard_map/ppermute | solution.py:57
  172.0 3.7 %collective-permute-done.15.got = bf16[144,2048]{1,0:T(8,128)(2,1)S(1)} collective-permute-done((bf16[144,2048]{1,0:T(8,128)(2,1)S(1)}, bf16[144,2048]{1,0:T(8,128)(2,1)S(1)}, u32[]{:S(2)}, u32[]{:S(2)}) %collective-permute-start.15) | collective-permute-done | bytes 589856 | tf_op jit(solution)/shard_map/ppermute | solution.py:57
  175.8 0.8 owner.2
  176.6 2.0 collective-permute-start.16
  178.5 10.0 %collective-permute-done.20.refs_4_ = bf16[144,512]{1,0:T(8,128)(2,1)S(1)} collective-permute-done((bf16[144,512]{1,0:T(8,128)(2,1)S(1)}, bf16[144,512]{1,0:T(8,128)(2,1)S(1)}, u32[]{:S(2)}, u32[]{:S(2)}) %collective-permute-start.20) | collective-permute-done | bytes 147488 | tf_op jit(solution)/shard_map/ppermute | solution.py:57
  188.5 4.0 %collective-permute-done.21.refs_5_ = bf16[144,512]{1,0:T(8,128)(2,1)S(1)} collective-permute-done((bf16[144,512]{1,0:T(8,128)(2,1)S(1)}, bf16[144,512]{1,0:T(8,128)(2,1)S(1)}, u32[]{:S(2)}, u32[]{:S(2)}) %collective-permute-start.21) | collective-permute-done | bytes 147488 | tf_op jit(solution)/shard_map/ppermute | solution.py:57
  192.5 1.1 reduce.1.refs_0_
  193.7 4.3 %all-to-all-start.3 = ((bf16[8,4,16,256]{3,2,1,0:T(8,128)(2,1)}), bf16[8,4,16,256]{3,2,1,0:T(8,128)(2,1)S(1)}, u32[]{:S(2)}, u32[]{:S(2)}) async-start(bf16[8,4,16,256]{3,2,1,0:T(8,128)(2,1)} %after.3), calls=%async_computation.3 | async-start | bytes 524288 | tf_op jit(solution)/shard_map/all_to_all | solution.py:61
  198.0 0.7 collective-permute-done.18.refs_3_
  198.8 2.0 scatter.1.refs_0_
  200.7 1.6 collective-permute-start.25
  202.3 5.2 %collective-permute-done.25.refs_2_ = bf16[144,1024]{1,0:T(8,128)(2,1)S(1)} collective-permute-done((bf16[144,1024]{1,0:T(8,128)(2,1)S(1)}, bf16[144,1024]{1,0:T(8,128)(2,1)S(1)}, u32[]{:S(2)}, u32[]{:S(2)}) %collective-permute-start.25) | collective-permute-done | bytes 294944 | tf_op jit(solution)/shard_map/ppermute | solution.py:57
  207.5 0.7 copy.33
  208.3 0.7 copy.31
  209.0 0.7 copy.32
  209.6 2.1 assemble.1
  (79 shorter events, 4.5 us)
Async XLA Ops:
  0.7 66.1 %copy-start.4 = (s32[2]{0:T(128)}, s32[2]{0:T(128)S(1)}, u32[]{:S(2)}) copy-start(s32[2]{0:T(128)S(1)} %pad_add_fusion.3.ids) | copy-start | bytes 28
  0.7 1.3 copy-start.1
  2.0 4.7 %copy-start.13 = (bf16[32,8192]{1,0:T(8,128)(2,1)S(1)}, bf16[32,8192]{1,0:T(8,128)(2,1)}, u32[]{:S(2)}) copy-start(bf16[32,8192]{1,0:T(8,128)(2,1)} %param.11) | copy-start | bytes 1572868
  2.6 4.6 %copy-start.14 = (bf16[32,8192]{1,0:T(8,128)(2,1)S(1)}, bf16[32,8192]{1,0:T(8,128)(2,1)}, u32[]{:S(2)}) copy-start(bf16[32,8192]{1,0:T(8,128)(2,1)} %param.12) | copy-start | bytes 1572868
  2.6 17.4 %collective-permute-start = (bf16[144,1024]{1,0:T(8,128)(2,1)S(1)}, bf16[144,1024]{1,0:T(8,128)(2,1)S(1)}, u32[]{:S(2)}, u32[]{:S(2)}) collective-permute-start(bf16[144,1024]{1,0:T(8,128)(2,1)S(1)} %cut.1.refs_0_), channel_id=1, source_target_pairs={{0,16},{4,20},{8,24},{12,28},{16,0},{20,4},{24,8},{28,12},{1,17},{... | collective-permute-start | bytes 884744 | tf_op jit(solution)/shard_map/ppermute | solution.py:57
  7.0 0.9 copy-start.17
  7.1 1.0 copy-start.18
  20.0 5.9 %copy-start.6 = (s32[1,64]{1,0:T(1,128)S(1)}, s32[1,64]{1,0:T(1,128)}, u32[]{:S(2)}) copy-start(s32[1,64]{1,0:T(1,128)} %own.1) | copy-start | bytes 772
  20.0 50.2 %all-to-all-start = ((bf16[32,160,128]{2,1,0:T(8,128)(2,1)}), bf16[32,160,128]{2,1,0:T(8,128)(2,1)S(1)}, u32[]{:S(2)}, u32[]{:S(2)}) async-start(bf16[32,160,128]{2,1,0:T(8,128)(2,1)} %after.2), calls=%async_computation | async-start | bytes 2621440 | tf_op jit(solution)/shard_map/all_to_all | solution.py:61
  25.9 10.1 %collective-permute-start.1 = (s32[1,64]{1,0:T(1,128)S(1)}, s32[1,64]{1,0:T(1,128)S(1)}, u32[]{:S(2)}, u32[]{:S(2)}) collective-permute-start(s32[1,64]{1,0:T(1,128)S(1)} %copy-done.6), channel_id=1, source_target_pairs={{0,4},{4,0},{8,12},{12,8},{16,20},{20,16},{24,28},{28,24},{1,5},{5... | collective-permute-start | bytes 776 | tf_op jit(solution)/shard_map/ppermute | solution.py:57
  27.9 38.9 %collective-permute-start.2 = (bf16[144,1024]{1,0:T(8,128)(2,1)S(1)}, bf16[144,1024]{1,0:T(8,128)(2,1)S(1)}, u32[]{:S(2)}, u32[]{:S(2)}) collective-permute-start(bf16[144,1024]{1,0:T(8,128)(2,1)S(1)} %cut.1.refs_0_), channel_id=1, source_target_pairs={{0,8},{4,12},{8,0},{12,4},{16,24},{20,28},{24,16},{28,20},{1,9},{5... | collective-permute-start | bytes 884744 | tf_op jit(solution)/shard_map/ppermute | solution.py:57
  29.4 37.4 %collective-permute-start.3 = (bf16[144,1024]{1,0:T(8,128)(2,1)S(1)}, bf16[144,1024]{1,0:T(8,128)(2,1)S(1)}, u32[]{:S(2)}, u32[]{:S(2)}) collective-permute-start(bf16[144,1024]{1,0:T(8,128)(2,1)S(1)} %collective-permute-done.refs_1_.refs_2_), channel_id=1, source_target_pairs={{0,8},{4,12},{8,0},{12,4},{16,24},{20,28},{24,16},{28,20},{1,9},{5... | collective-permute-start | bytes 884744 | tf_op jit(solution)/shard_map/ppermute | solution.py:57
  36.0 26.3 %collective-permute-start.4 = (s32[2,64]{1,0:T(2,128)S(1)}, s32[2,64]{1,0:T(2,128)S(1)}, u32[]{:S(2)}, u32[]{:S(2)}) collective-permute-start(s32[2,64]{1,0:T(2,128)S(1)} %pad_add_fusion.2), channel_id=1, source_target_pairs={{0,8},{4,12},{8,0},{12,4},{16,24},{20,28},{24,16},{28,20},{1,9},{5... | collective-permute-start | bytes 1544 | tf_op jit(solution)/shard_map/ppermute | solution.py:57
  62.3 4.5 %collective-permute-start.5 = (s32[4,64]{1,0:T(4,128)S(1)}, s32[4,64]{1,0:T(4,128)S(1)}, u32[]{:S(2)}, u32[]{:S(2)}) collective-permute-start(s32[4,64]{1,0:T(4,128)S(1)} %pad_add_fusion.1.refs_4_), channel_id=1, source_target_pairs={{0,16},{4,20},{8,24},{12,28},{16,0},{20,4},{24,8},{28,12},{1,17},{... | collective-permute-start | bytes 3080 | tf_op jit(solution)/shard_map/ppermute | solution.py:57
  70.2 31.8 %copy-start.3 = (bf16[144,2048]{1,0:T(8,128)(2,1)}, bf16[144,2048]{1,0:T(8,128)(2,1)S(1)}, u32[]{:S(2)}) copy-start(bf16[144,2048]{1,0:T(8,128)(2,1)S(1)} %get-tuple-element.26.refs_0_) | copy-start | bytes 1769476
  71.6 41.8 %copy-start.15 = (bf16[16,32,64]{2,1,0:T(8,128)(2,1)S(1)}, bf16[16,32,64]{2,1,0:T(8,128)(2,1)}, u32[]{:S(2)}) copy-start(bf16[16,32,64]{2,1,0:T(8,128)(2,1)} %param.9) | copy-start | bytes 196612
  71.6 44.5 %all-to-all-start.1 = ((bf16[8,4,16,1024]{3,2,1,0:T(8,128)(2,1)}), bf16[8,4,16,1024]{3,2,1,0:T(8,128)(2,1)}, u32[]{:S(2)}, u32[]{:S(2)}) async-start(bf16[8,4,16,1024]{3,2,1,0:T(8,128)(2,1)} %expand.1), calls=%async_computation.1 | async-start | bytes 2097152 | tf_op jit(solution)/shard_map/all_to_all | solution.py:61
  76.4 24.1 %collective-permute-start.9 = (bf16[144,2048]{1,0:T(8,128)(2,1)S(1)}, bf16[144,2048]{1,0:T(8,128)(2,1)S(1)}, u32[]{:S(2)}, u32[]{:S(2)}) collective-permute-start(bf16[144,2048]{1,0:T(8,128)(2,1)S(1)} %get-tuple-element.25.away), channel_id=1, source_target_pairs={{0,4},{4,0},{8,12},{12,8},{16,20},{20,16},{24,28},{28,24},{1,5},{5... | collective-permute-start | bytes 1769480 | tf_op jit(solution)/shard_map/ppermute | solution.py:57
  78.4 24.1 %collective-permute-start.7 = (bf16[144,2048]{1,0:T(8,128)(2,1)S(1)}, bf16[144,2048]{1,0:T(8,128)(2,1)S(1)}, u32[]{:S(2)}, u32[]{:S(2)}) collective-permute-start(bf16[144,2048]{1,0:T(8,128)(2,1)S(1)} %get-tuple-element.26.refs_0_), channel_id=1, source_target_pairs={{0,2},{1,3},{2,0},{3,1},{4,6},{5,7},{6,4},{7,5},{8,10},{9,11},{10,... | collective-permute-start | bytes 1769480 | tf_op jit(solution)/shard_map/ppermute | solution.py:57
  100.5 15.7 %copy-start.7 = (bf16[144,2048]{1,0:T(8,128)(2,1)}, bf16[144,2048]{1,0:T(8,128)(2,1)S(1)}, u32[]{:S(2)}) copy-start(bf16[144,2048]{1,0:T(8,128)(2,1)S(1)} %collective-permute-done.9.refs_4_) | copy-start | bytes 1769476
  100.5 13.0 %collective-permute-start.11 = (bf16[144,2048]{1,0:T(8,128)(2,1)S(1)}, bf16[144,2048]{1,0:T(8,128)(2,1)S(1)}, u32[]{:S(2)}, u32[]{:S(2)}) collective-permute-start(bf16[144,2048]{1,0:T(8,128)(2,1)S(1)} %collective-permute-done.9.refs_4_), channel_id=1, source_target_pairs={{0,2},{1,3},{2,0},{3,1},{4,6},{5,7},{6,4},{7,5},{8,10},{9,11},{10,... | collective-permute-start | bytes 1769480 | tf_op jit(solution)/shard_map/ppermute | solution.py:57
  102.0 12.3 %collective-permute-start.6 = (bf16[144,2048]{1,0:T(8,128)(2,1)S(1)}, bf16[144,2048]{1,0:T(8,128)(2,1)S(1)}, u32[]{:S(2)}, u32[]{:S(2)}) collective-permute-start(bf16[144,2048]{1,0:T(8,128)(2,1)S(1)} %get-tuple-element.26.refs_0_), channel_id=1, source_target_pairs={{0,1},{1,0},{2,3},{3,2},{4,5},{5,4},{6,7},{7,6},{8,9},{9,8},{10,11... | collective-permute-start | bytes 1769480 | tf_op jit(solution)/shard_map/ppermute | solution.py:57
  102.0 12.3 %collective-permute-start.10 = (bf16[144,2048]{1,0:T(8,128)(2,1)S(1)}, bf16[144,2048]{1,0:T(8,128)(2,1)S(1)}, u32[]{:S(2)}, u32[]{:S(2)}) collective-permute-start(bf16[144,2048]{1,0:T(8,128)(2,1)S(1)} %collective-permute-done.9.refs_4_), channel_id=1, source_target_pairs={{0,1},{1,0},{2,3},{3,2},{4,5},{5,4},{6,7},{7,6},{8,9},{9,8},{10,11... | collective-permute-start | bytes 1769480 | tf_op jit(solution)/shard_map/ppermute | solution.py:57
  102.5 11.8 %copy-start.8 = (bf16[144,2048]{1,0:T(8,128)(2,1)}, bf16[144,2048]{1,0:T(8,128)(2,1)S(1)}, u32[]{:S(2)}) copy-start(bf16[144,2048]{1,0:T(8,128)(2,1)S(1)} %collective-permute-done.7.refs_2_) | copy-start | bytes 1769476
  102.5 11.8 %collective-permute-start.8 = (bf16[144,2048]{1,0:T(8,128)(2,1)S(1)}, bf16[144,2048]{1,0:T(8,128)(2,1)S(1)}, u32[]{:S(2)}, u32[]{:S(2)}) collective-permute-start(bf16[144,2048]{1,0:T(8,128)(2,1)S(1)} %collective-permute-done.7.refs_2_), channel_id=1, source_target_pairs={{0,1},{1,0},{2,3},{3,2},{4,5},{5,4},{6,7},{7,6},{8,9},{9,8},{10,11... | collective-permute-start | bytes 1769480 | tf_op jit(solution)/shard_map/ppermute | solution.py:57
  113.4 2.7 %copy-start.9 = (bf16[144,2048]{1,0:T(8,128)(2,1)}, bf16[144,2048]{1,0:T(8,128)(2,1)S(1)}, u32[]{:S(2)}) copy-start(bf16[144,2048]{1,0:T(8,128)(2,1)S(1)} %collective-permute-done.11.refs_6_) | copy-start | bytes 1769476
  113.4 2.7 %collective-permute-start.12 = (bf16[144,2048]{1,0:T(8,128)(2,1)S(1)}, bf16[144,2048]{1,0:T(8,128)(2,1)}, u32[]{:S(2)}, u32[]{:S(2)}) collective-permute-start(bf16[144,2048]{1,0:T(8,128)(2,1)S(1)} %collective-permute-done.11.refs_6_), channel_id=1, source_target_pairs={{0,1},{1,0},{2,3},{3,2},{4,5},{5,4},{6,7},{7,6},{8,9},{9,8},{10,11... | collective-permute-start | bytes 1769480 | tf_op jit(solution)/shard_map/ppermute | solution.py:57
  114.2 1.0 copy-start.11
  139.3 6.3 %copy-start = (bf16[2,144,2048]{2,1,0:T(8,128)(2,1)S(1)}, bf16[2,144,2048]{2,1,0:T(8,128)(2,1)}, u32[]{:S(2)}) copy-start(bf16[2,144,2048]{2,1,0:T(8,128)(2,1)} %get-tuple-element.28.keep) | copy-start | bytes 3538948
  139.3 6.3 %collective-permute-start.13 = (bf16[2,144,2048]{2,1,0:T(8,128)(2,1)}, bf16[2,144,2048]{2,1,0:T(8,128)(2,1)}, u32[]{:S(2)}, u32[]{:S(2)}) collective-permute-start(bf16[2,144,2048]{2,1,0:T(8,128)(2,1)} %get-tuple-element.29), channel_id=1, source_target_pairs={{0,1},{1,0},{2,3},{3,2},{4,5},{5,4},{6,7},{7,6},{8,9},{9,8},{10,11... | collective-permute-start | bytes 3538952 | tf_op jit(solution)/shard_map/ppermute | solution.py:57
  139.8 52.7 %all-to-all-start.2 = ((bf16[8,4,16,1024]{3,2,1,0:T(8,128)(2,1)}), bf16[8,4,16,1024]{3,2,1,0:T(8,128)(2,1)S(1)}, u32[]{:S(2)}, u32[]{:S(2)}) async-start(bf16[8,4,16,1024]{3,2,1,0:T(8,128)(2,1)} %bitcast.36), calls=%async_computation.2 | async-start | bytes 2097152 | tf_op jit(solution)/shard_map/all_to_all | solution.py:61
  145.6 3.4 %copy-start.2 = (bf16[2,144,2048]{2,1,0:T(8,128)(2,1)S(1)}, bf16[2,144,2048]{2,1,0:T(8,128)(2,1)}, u32[]{:S(2)}) copy-start(bf16[2,144,2048]{2,1,0:T(8,128)(2,1)} %get-tuple-element.31.refs_1_) | copy-start | bytes 3538948
  145.6 3.4 %collective-permute-start.14 = (bf16[2,144,2048]{2,1,0:T(8,128)(2,1)}, bf16[2,144,2048]{2,1,0:T(8,128)(2,1)S(1)}, u32[]{:S(2)}, u32[]{:S(2)}) collective-permute-start(bf16[2,144,2048]{2,1,0:T(8,128)(2,1)} %get-tuple-element.32), channel_id=1, source_target_pairs={{0,1},{1,0},{2,3},{3,2},{4,5},{5,4},{6,7},{7,6},{8,9},{9,8},{10,11... | collective-permute-start | bytes 3538952 | tf_op jit(solution)/shard_map/ppermute | solution.py:57
  147.4 16.2 %collective-permute-start.19 = (bf16[144,2048]{1,0:T(8,128)(2,1)S(1)}, bf16[144,2048]{1,0:T(8,128)(2,1)S(1)}, u32[]{:S(2)}, u32[]{:S(2)}) collective-permute-start(bf16[144,2048]{1,0:T(8,128)(2,1)S(1)} %get-tuple-element.41), channel_id=1, source_target_pairs={{0,2},{1,3},{2,0},{3,1},{4,6},{5,7},{6,4},{7,5},{8,10},{9,11},{10,... | collective-permute-start | bytes 1769480 | tf_op jit(solution)/shard_map/ppermute | solution.py:57
  149.2 26.5 %collective-permute-start.15 = (bf16[144,2048]{1,0:T(8,128)(2,1)S(1)}, bf16[144,2048]{1,0:T(8,128)(2,1)S(1)}, u32[]{:S(2)}, u32[]{:S(2)}) collective-permute-start(bf16[144,2048]{1,0:T(8,128)(2,1)S(1)} %get-tuple-element.34), channel_id=1, source_target_pairs={{0,2},{1,3},{2,0},{3,1},{4,6},{5,7},{6,4},{7,5},{8,10},{9,11},{10,... | collective-permute-start | bytes 1769480 | tf_op jit(solution)/shard_map/ppermute | solution.py:57
  164.4 24.2 %collective-permute-start.20 = (bf16[144,512]{1,0:T(8,128)(2,1)S(1)}, bf16[144,512]{1,0:T(8,128)(2,1)S(1)}, u32[]{:S(2)}, u32[]{:S(2)}) collective-permute-start(bf16[144,512]{1,0:T(8,128)(2,1)S(1)} %get-tuple-element.42), channel_id=1, source_target_pairs={{0,16},{4,20},{8,24},{12,28},{16,0},{20,4},{24,8},{28,12},{1,17},{... | collective-permute-start | bytes 442376 | tf_op jit(solution)/shard_map/ppermute | solution.py:57
  167.2 25.3 %collective-permute-start.21 = (bf16[144,512]{1,0:T(8,128)(2,1)S(1)}, bf16[144,512]{1,0:T(8,128)(2,1)S(1)}, u32[]{:S(2)}, u32[]{:S(2)}) collective-permute-start(bf16[144,512]{1,0:T(8,128)(2,1)S(1)} %get-tuple-element.43), channel_id=1, source_target_pairs={{0,20},{4,16},{8,28},{12,24},{16,4},{20,0},{24,12},{28,8},{1,21},{... | collective-permute-start | bytes 442376 | tf_op jit(solution)/shard_map/ppermute | solution.py:57
  168.7 29.3 %collective-permute-start.22 = (bf16[144,512]{1,0:T(8,128)(2,1)}, bf16[144,512]{1,0:T(8,128)(2,1)S(1)}, u32[]{:S(2)}, u32[]{:S(2)}) collective-permute-start(bf16[144,512]{1,0:T(8,128)(2,1)} %get-tuple-element.44), channel_id=1, source_target_pairs={{0,24},{4,28},{8,16},{12,20},{16,8},{20,12},{24,0},{28,4},{1,25},{... | collective-permute-start | bytes 442376 | tf_op jit(solution)/shard_map/ppermute | solution.py:57
  172.0 26.0 %collective-permute-start.23 = (bf16[144,512]{1,0:T(8,128)(2,1)}, bf16[144,512]{1,0:T(8,128)(2,1)S(1)}, u32[]{:S(2)}, u32[]{:S(2)}) collective-permute-start(bf16[144,512]{1,0:T(8,128)(2,1)} %get-tuple-element.45), channel_id=1, source_target_pairs={{0,28},{4,24},{8,20},{12,16},{16,12},{20,8},{24,4},{28,0},{1,29},{... | collective-permute-start | bytes 442376 | tf_op jit(solution)/shard_map/ppermute | solution.py:57
  176.6 21.5 %collective-permute-start.16 = (bf16[144,512]{1,0:T(8,128)(2,1)}, bf16[144,512]{1,0:T(8,128)(2,1)S(1)}, u32[]{:S(2)}, u32[]{:S(2)}) collective-permute-start(bf16[144,512]{1,0:T(8,128)(2,1)} %get-tuple-element.37), channel_id=1, source_target_pairs={{0,4},{4,0},{8,12},{12,8},{16,20},{20,16},{24,28},{28,24},{1,5},{5... | collective-permute-start | bytes 442376 | tf_op jit(solution)/shard_map/ppermute | solution.py:57
  188.5 9.5 %collective-permute-start.17 = (bf16[144,512]{1,0:T(8,128)(2,1)}, bf16[144,512]{1,0:T(8,128)(2,1)S(1)}, u32[]{:S(2)}, u32[]{:S(2)}) collective-permute-start(bf16[144,512]{1,0:T(8,128)(2,1)} %get-tuple-element.38), channel_id=1, source_target_pairs={{0,8},{4,12},{8,0},{12,4},{16,24},{20,28},{24,16},{28,20},{1,9},{5... | collective-permute-start | bytes 442376 | tf_op jit(solution)/shard_map/ppermute | solution.py:57
  192.5 6.3 %copy-start.5 = (s32[2]{0:T(128)S(1)}, s32[2]{0:T(128)}, u32[]{:S(2)}) copy-start(s32[2]{0:T(128)} %copy-done.4) | copy-start | bytes 28
  192.5 6.3 %collective-permute-start.18 = (bf16[144,512]{1,0:T(8,128)(2,1)}, bf16[144,512]{1,0:T(8,128)(2,1)S(1)}, u32[]{:S(2)}, u32[]{:S(2)}) collective-permute-start(bf16[144,512]{1,0:T(8,128)(2,1)} %get-tuple-element.39), channel_id=1, source_target_pairs={{0,12},{4,8},{8,4},{12,0},{16,28},{20,24},{24,20},{28,16},{1,13},{... | collective-permute-start | bytes 442376 | tf_op jit(solution)/shard_map/ppermute | solution.py:57
  193.7 13.9 %copy-start.16 = (bf16[512,64]{1,0:T(8,128)(2,1)S(1)}, bf16[512,64]{1,0:T(8,128)(2,1)}, u32[]{:S(2)}) copy-start(bf16[512,64]{1,0:T(8,128)(2,1)} %get-tuple-element.36) | copy-start | bytes 196612
  193.7 14.5 %all-to-all-start.3 = ((bf16[8,4,16,256]{3,2,1,0:T(8,128)(2,1)}), bf16[8,4,16,256]{3,2,1,0:T(8,128)(2,1)S(1)}, u32[]{:S(2)}, u32[]{:S(2)}) async-start(bf16[8,4,16,256]{3,2,1,0:T(8,128)(2,1)} %after.3), calls=%async_computation.3 | async-start | bytes 524288 | tf_op jit(solution)/shard_map/all_to_all | solution.py:61
  200.7 6.8 %collective-permute-start.25 = (bf16[144,1024]{1,0:T(8,128)(2,1)S(1)}, bf16[144,1024]{1,0:T(8,128)(2,1)S(1)}, u32[]{:S(2)}, u32[]{:S(2)}) collective-permute-start(bf16[144,1024]{1,0:T(8,128)(2,1)S(1)} %scatter.1.refs_0_), channel_id=1, source_target_pairs={{0,2},{1,3},{2,0},{3,1},{4,6},{5,7},{6,4},{7,5},{8,10},{9,11},{10,... | collective-permute-start | bytes 884744 | tf_op jit(solution)/shard_map/ppermute | solution.py:57
  202.3 7.4 %collective-permute-start.24 = (bf16[144,1024]{1,0:T(8,128)(2,1)S(1)}, bf16[144,1024]{1,0:T(8,128)(2,1)S(1)}, u32[]{:S(2)}, u32[]{:S(2)}) collective-permute-start(bf16[144,1024]{1,0:T(8,128)(2,1)S(1)} %scatter.1.refs_0_), channel_id=1, source_target_pairs={{0,1},{1,0},{2,3},{3,2},{4,5},{5,4},{6,7},{7,6},{8,9},{9,8},{10,11... | collective-permute-start | bytes 884744 | tf_op jit(solution)/shard_map/ppermute | solution.py:57
  207.5 2.1 %collective-permute-start.26 = (bf16[144,1024]{1,0:T(8,128)(2,1)S(1)}, bf16[144,1024]{1,0:T(8,128)(2,1)S(1)}, u32[]{:S(2)}, u32[]{:S(2)}) collective-permute-start(bf16[144,1024]{1,0:T(8,128)(2,1)S(1)} %collective-permute-done.25.refs_2_), channel_id=1, source_target_pairs={{0,1},{1,0},{2,3},{3,2},{4,5},{5,4},{6,7},{7,6},{8,9},{9,8},{10,11... | collective-permute-start | bytes 884744 | tf_op jit(solution)/shard_map/ppermute | solution.py:57
  (2 other events, 1.7 us)
